TPU v7x, 32 devices: a whole 2x2x4 slice. The times are simulated.
32 devices in a mesh: img: 8 (over y, x, core), lat: 4 (over z).
Axes of the slice: x: 2, y: 2, z: 4, core: 2. Of those that a mesh axis runs over, the one named last changes fastest.
Arguments:
- latents: bfloat16 [48, 512, 1024], P('img', 'lat'), may hold values from -6 to 6
- pixels: bfloat16 [48, 4096, 261], P('img', 'lat'), may hold values from -6 to 6
- keep_mask: int32 [48, 4096], P('img', 'lat'), may hold values from 0 to 1, as said below
- cotangent: bfloat16 [48, 512, 1024], P('img', 'lat'), may hold values from -6 to 6
- gain_latent: float32 [1024], replicated, may hold values from 0.1 to 1.9
- gain_pixel: float32 [261], replicated, may hold values from 0.1 to 1.9
- gain_mlp: float32 [1024], replicated, may hold values from 0.1 to 1.9
- w_query: bfloat16 [1024, 1024], P(('img', 'lat')), may hold values from -0.1875 to 0.1875
- w_key: bfloat16 [261, 1024], P(None, ('img', 'lat')), may hold values from -0.375 to 0.375
- w_value: bfloat16 [261, 1024], P(None, ('img', 'lat')), may hold values from -0.375 to 0.375
- w_output: bfloat16 [1024, 1024], P(('img', 'lat')), may hold values from -6 to 6
- w_hidden: bfloat16 [1024, 1024], P(('img', 'lat')), may hold values from -0.1875 to 0.1875
- w_return: bfloat16 [1024, 1024], P(('img', 'lat')), may hold values from -0.1875 to 0.1875
Outputs:
- output: bfloat16 [48, 512, 1024], P('img', 'lat')
- grad_latents: bfloat16 [48, 512, 1024], P('img', 'lat')
- grad_pixels: bfloat16 [48, 4096, 261], P('img', 'lat')
- grad_query: float32 [1024, 1024], P(('img', 'lat'))
- grad_key: float32 [261, 1024], P(None, ('img', 'lat'))
- grad_value: float32 [261, 1024], P(None, ('img', 'lat'))
- grad_output: float32 [1024, 1024], P(('img', 'lat'))
- grad_hidden: float32 [1024, 1024], P(('img', 'lat'))
- grad_return: float32 [1024, 1024], P(('img', 'lat'))
- grad_gain_latent: float32 [1024], replicated
- grad_gain_pixel: float32 [261], replicated
- grad_gain_mlp: float32 [1024], replicated
Inputs may be any that keep to these rules, and one draw needn't show every extreme that they name: `keep_mask`: values 0 or 1; each image keeps between 30 and 95 percent of its 4096 pixels.
All inputs are finite; a program needn't handle non-finite values.
Results may differ from a plain program's by a relative error of at most 0.017.
Values may be sent and summed in bfloat16 or wider, within the bound.
No kernel may reach another device: no remote copies, remote signals or barrier semaphores. Data moves between devices by JAX's collectives and lax.ppermute only.
A program may use at most 320 MiB of HBM per device.

v0:
```python
from functools import partial

import jax
import jax.numpy as jnp
from jax import lax
from jax.sharding import PartitionSpec as P


def normalize(values):
    centered = values - jnp.mean(values, -1, keepdims=True)
    rstd = lax.rsqrt(jnp.mean(centered * centered, -1, keepdims=True) + 1e-05)
    return (centered * rstd, rstd)


def norm_back(upstream, normed, rstd):
    return rstd * (
        upstream
        - jnp.mean(upstream, -1, keepdims=True)
        - normed * jnp.mean(upstream * normed, -1, keepdims=True)
    )


def split_parts(values):
    upper = values.astype(jnp.bfloat16)
    lower = (values - upper.astype(jnp.float32)).astype(jnp.bfloat16)
    return (upper, lower)


def split_product(form, wide, narrow):
    upper, lower = split_parts(narrow)
    first = jnp.einsum(form, wide, upper, preferred_element_type=jnp.float32)
    return first + jnp.einsum(form, wide, lower, preferred_element_type=jnp.float32)


def local(
    latents,
    pixels,
    keep_mask,
    cotangent,
    gain_latent,
    gain_pixel,
    gain_mlp,
    w_query,
    w_key,
    w_value,
    w_output,
    w_hidden,
    w_return,
):
    f32 = jnp.float32
    bf16 = jnp.bfloat16
    wq, wk, wv, wo, w1, w2 = (
        lax.all_gather(w_query, ("img", "lat"), axis=0, tiled=True),
        lax.all_gather(w_key, ("img", "lat"), axis=1, tiled=True),
        lax.all_gather(w_value, ("img", "lat"), axis=1, tiled=True),
        lax.all_gather(w_output, ("img", "lat"), axis=0, tiled=True),
        lax.all_gather(w_hidden, ("img", "lat"), axis=0, tiled=True),
        lax.all_gather(w_return, ("img", "lat"), axis=0, tiled=True),
    )
    scale = wq.shape[0] ** (-0.5)
    lat_f = latents.astype(f32)
    lat_hat, lat_rstd = normalize(lat_f)
    lat_in = (lat_hat * gain_latent).astype(bf16)
    pix_hat, pix_rstd = normalize(pixels.astype(f32))
    pix_in = (pix_hat * gain_pixel).astype(bf16)
    all_pix, all_keep = (
        lax.all_gather(pix_in, "lat", axis=1, tiled=True),
        lax.all_gather(keep_mask.astype(bf16), "lat", axis=1, tiled=True),
    )
    visible = all_keep > 0.5
    query = jnp.einsum("bld,de->ble", lat_in, wq, preferred_element_type=f32).astype(bf16)
    keys = jnp.einsum("bmc,cd->bmd", all_pix, wk, preferred_element_type=f32).astype(bf16)
    vals = jnp.einsum("bmc,cd->bmd", all_pix, wv, preferred_element_type=f32).astype(bf16)

    def masked_scores():
        raw = jnp.einsum("bld,bmd->blm", query, keys, preferred_element_type=f32) * scale
        return jnp.where(visible[:, None, :], raw, -jnp.inf)

    scores = masked_scores()
    top = jnp.max(scores, -1, keepdims=True)
    expo = jnp.exp(scores - top)
    total = jnp.sum(expo, -1, keepdims=True)
    log_total = top + jnp.log(total)
    probs_low = (expo / total).astype(bf16)
    attended = jnp.einsum("blm,bmd->bld", probs_low, vals, preferred_element_type=f32).astype(bf16)
    middle = lat_f + jnp.einsum("bld,de->ble", attended, wo, preferred_element_type=f32)
    mid_hat, mid_rstd = normalize(middle)
    mlp_in = (mid_hat * gain_mlp).astype(bf16)
    pre = jnp.einsum("bld,de->ble", mlp_in, w1, preferred_element_type=f32)
    act, gelu_back = jax.vjp(partial(jax.nn.gelu, approximate=False), pre)
    act_low = act.astype(bf16)
    result = middle + jnp.einsum("bld,de->ble", act_low, w2, preferred_element_type=f32)
    output = result.astype(bf16)
    wq, wk, wv, wo, w1, w2 = (
        lax.all_gather(w_query, ("img", "lat"), axis=0, tiled=True),
        lax.all_gather(w_key, ("img", "lat"), axis=1, tiled=True),
        lax.all_gather(w_value, ("img", "lat"), axis=1, tiled=True),
        lax.all_gather(w_output, ("img", "lat"), axis=0, tiled=True),
        lax.all_gather(w_hidden, ("img", "lat"), axis=0, tiled=True),
        lax.all_gather(w_return, ("img", "lat"), axis=0, tiled=True),
    )
    grad_return = jnp.einsum("bli,blj->ij", act_low, cotangent, preferred_element_type=f32)
    grad_act = jnp.einsum("blj,ij->bli", cotangent, w2, preferred_element_type=f32)
    grad_pre = gelu_back(grad_act)[0].astype(bf16)
    grad_hidden = jnp.einsum("bli,blj->ij", mlp_in, grad_pre, preferred_element_type=f32)
    grad_mlp_in = jnp.einsum("blj,ij->bli", grad_pre, w1, preferred_element_type=f32)
    grad_gain_mlp = jnp.sum(grad_mlp_in * mid_hat, (0, 1))
    grad_middle = cotangent.astype(f32) + norm_back(grad_mlp_in * gain_mlp, mid_hat, mid_rstd)
    grad_branch = grad_middle.astype(bf16)
    grad_output = jnp.einsum("bli,blj->ij", attended, grad_branch, preferred_element_type=f32)
    grad_att = jnp.einsum("blj,ij->bli", grad_branch, wo, preferred_element_type=f32).astype(bf16)
    probs = jnp.exp(masked_scores() - log_total)
    probs_again = probs.astype(bf16)
    grad_probs = jnp.einsum("bld,bmd->blm", grad_att, vals, preferred_element_type=f32)
    inner = jnp.sum(grad_probs * probs, -1, keepdims=True)
    grad_scores = (probs * (grad_probs - inner)).astype(bf16)
    grad_q = (
        jnp.einsum("blm,bmd->bld", grad_scores, keys, preferred_element_type=f32) * scale
    ).astype(bf16)
    grad_query = jnp.einsum("bld,ble->de", lat_in, grad_q, preferred_element_type=f32)
    grad_lat_in = jnp.einsum("ble,de->bld", grad_q, wq, preferred_element_type=f32)
    both_rows = jnp.concatenate([grad_scores, probs_again], axis=1)
    pix_terms = jnp.einsum("blm,bmc->blc", both_rows, all_pix, preferred_element_type=f32)
    rows = grad_scores.shape[1]
    grad_key = split_product("bld,blc->cd", query, pix_terms[:, :rows]) * scale
    grad_value = split_product("bld,blc->cd", grad_att, pix_terms[:, rows:])
    query_key = jnp.einsum("bld,cd->blc", query, wk, preferred_element_type=f32) * scale
    att_value = jnp.einsum("bld,cd->blc", grad_att, wv, preferred_element_type=f32)
    side_terms = jnp.concatenate([query_key, att_value], axis=1)
    grad_pix_all = split_product("blm,blc->bmc", both_rows, side_terms)
    grad_pix_in = lax.psum_scatter(
        grad_pix_all.astype(jnp.bfloat16), "lat", scatter_dimension=1, tiled=True
    ).astype(jnp.float32)
    grad_gain_pixel = jnp.sum(grad_pix_in * pix_hat, (0, 1))
    grad_pixels = norm_back(grad_pix_in * gain_pixel, pix_hat, pix_rstd).astype(bf16)
    grad_gain_latent = jnp.sum(grad_lat_in * lat_hat, (0, 1))
    grad_latents = (grad_middle + norm_back(grad_lat_in * gain_latent, lat_hat, lat_rstd)).astype(
        bf16
    )
    shard_q, shard_k, shard_v, shard_o, shard_h, shard_r = (
        lax.psum_scatter(grad_query, ("img", "lat"), scatter_dimension=0, tiled=True),
        lax.psum_scatter(grad_key, ("img", "lat"), scatter_dimension=1, tiled=True),
        lax.psum_scatter(grad_value, ("img", "lat"), scatter_dimension=1, tiled=True),
        lax.psum_scatter(grad_output, ("img", "lat"), scatter_dimension=0, tiled=True),
        lax.psum_scatter(grad_hidden, ("img", "lat"), scatter_dimension=0, tiled=True),
        lax.psum_scatter(grad_return, ("img", "lat"), scatter_dimension=0, tiled=True),
    )
    sum_lat, sum_pix, sum_mlp = lax.psum(
        (grad_gain_latent, grad_gain_pixel, grad_gain_mlp), ("img", "lat")
    )
    return (
        output,
        grad_latents,
        grad_pixels,
        shard_q,
        shard_k,
        shard_v,
        shard_o,
        shard_h,
        shard_r,
        sum_lat,
        sum_pix,
        sum_mlp,
    )


def solution(mesh):
    in_specs = (
        P("img", "lat", None),
        P("img", "lat", None),
        P("img", "lat"),
        P("img", "lat", None),
        P(),
        P(),
        P(),
        P(("img", "lat"), None),
        P(None, ("img", "lat")),
        P(None, ("img", "lat")),
        P(("img", "lat"), None),
        P(("img", "lat"), None),
        P(("img", "lat"), None),
    )
    out_specs = (
        P("img", "lat", None),
        P("img", "lat", None),
        P("img", "lat", None),
        P(("img", "lat"), None),
        P(None, ("img", "lat")),
        P(None, ("img", "lat")),
        P(("img", "lat"), None),
        P(("img", "lat"), None),
        P(("img", "lat"), None),
        P(),
        P(),
        P(),
    )
    return jax.shard_map(local, mesh=mesh, in_specs=in_specs, out_specs=out_specs, check_vma=False)
```

profile of v0, /device:TPU:0, one launch (start us, length us, event | category | flops | bytes accessed | tf_op | source)
XLA Modules:
  0.0 1611.7 jit_solution(17242548510247774370)
XLA Ops:
  7.2 0.7 all-gather.6.cloned.1.call-update
  8.0 2.7 convert_reduce_fusion
  10.8 0.9 fusion.13
  11.7 0.6 copy-done.24
  12.3 2.9 fusion.9
  15.3 0.7 all-gather.10.cloned.1.call-update
  16.0 0.5 all-gather.12.cloned.1.call-update
  16.6 0.5 all-gather.14.cloned.1.call-update
  17.2 0.3 convert_reduce_fusion.1
  17.5 0.5 fusion.34
  18.1 14.9 all_gather.30
  33.1 88.5 %all_gather.33 = bf16[261,1024]{0,1:T(8,128)(2,1)} all-gather(bf16[261,32]{0,1:T(8,128)(2,1)S(1)} %copy-done.29), channel_id=1, replica_groups=mesh['img'=8,'lat'=4] {'img','lat'}, dimensions={1}, use_global_device_ids=true | all-gather | bytes 551232 | tf_op jit(solution)/shard_map/all_gather | solution.py:54
  121.6 118.3 %all_gather.34 = bf16[261,1024]{0,1:T(8,128)(2,1)} all-gather(bf16[261,32]{0,1:T(8,128)(2,1)S(1)} %copy-done.30), channel_id=1, replica_groups=mesh['img'=8,'lat'=4] {'img','lat'}, dimensions={1}, use_global_device_ids=true | all-gather | bytes 551232 | tf_op jit(solution)/shard_map/all_gather | solution.py:55
  239.9 3.5 fusion.61
  243.4 1.6 convolution_multiply_fusion
  245.0 71.8 %all-gather.8.cloned.1.call-done = bf16[6,4096,261]{1,2,0:T(8,128)(2,1)} async-done(((bf16[6,1024,261]{1,2,0:T(8,128)(2,1)}), bf16[6,4096,261]{1,2,0:T(8,128)(2,1)}) %all-gather.8.cloned.1.call-update) | async-done | bytes 12828688 | tf_op jit(solution)/shard_map/all_gather | solution.py:67
  316.8 33.9 %convolution_convert_fusion.1 = bf16[6,4096,1024]{2,1,0:T(8,128)(2,1)} fusion(bf16[6,4096,261]{1,2,0:T(8,128)(2,1)} %all-gather.8.cloned.1.call-done, bf16[261,1024]{0,1:T(8,128)(2,1)S(1)} %copy-done.19), kind=kOutput, calls=%fused_computation.1 | convolution fusion | flops 13161725952 | bytes 63694848 | tf_op jit(solution)/shard_map/bmc,cd->bmd/dot_general | solution.py:72
  350.7 25.9 %fusion.92 = (f32[6,128]{1,0:T(8,128)S(1)}, f32[6,128,4096]{2,1,0:T(8,128)}) fusion(bf16[6,128,1024]{2,1,0:T(8,128)(2,1)S(1)} %fusion.61, bf16[6,4096,1024]{2,1,0:T(8,128)(2,1)} %convolution_convert_fusion.1, pred[6,4096]{1,0:T(8,128)(4,1)S(1)} %broadcast_compare_fusion), kind=kOutput, calls=%fused_computation.147 | convolution fusion | flops 6451887104 | bytes 64515072 | tf_op jit(solution)/shard_map/bld,bmd->blm/dot_general | solution.py:76
  376.6 6.4 fusion
  383.0 33.8 %convolution_convert_fusion = bf16[6,4096,1024]{2,1,0:T(8,128)(2,1)} fusion(bf16[6,4096,261]{1,2,0:T(8,128)(2,1)} %all-gather.8.cloned.1.call-done, bf16[261,1024]{0,1:T(8,128)(2,1)S(1)} %copy-done.16), kind=kOutput, calls=%fused_computation | convolution fusion | flops 13161725952 | bytes 63694848 | tf_op jit(solution)/shard_map/bmc,cd->bmd/dot_general | solution.py:73
  416.9 22.6 %fusion.67 = bf16[6,128,1024]{2,1,0:T(8,128)(2,1)S(1)} fusion(bf16[6,4096,1024]{2,1,0:T(8,128)(2,1)} %convolution_convert_fusion, f32[6,128,4096]{2,1,0:T(8,128)} %get-tuple-element.31, f32[6,128]{1,0:T(8,128)S(1)} %fusion, f32[6,128]{1,0:T(8,128)S(1)} %get-tuple-element.30), kind=kOutput, calls=%fused_computation.105 | convolution fusion | flops 6452674560 | bytes 64493568 | tf_op jit(solution)/shard_map/blm,bmd->bld/dot_general | solution.py:85
  439.5 4.0 fusion.93
  443.6 1.6 copy-done.7
  445.2 0.4 multiply_reduce_fusion.3
  445.7 5.2 fusion.83
  450.9 8.0 multiply_convert_fusion.2
  458.9 31.9 %all-gather.14.cloned.1.call-done = bf16[1024,1024]{1,0:T(8,128)(2,1)} async-done(((bf16[32,1024]{1,0:T(8,128)(2,1)}), bf16[1024,1024]{1,0:T(8,128)(2,1)}) %all-gather.14.cloned.1.call-update) | async-done | bytes 2097168 | tf_op jit(solution)/shard_map/all_gather | solution.py:58
  490.8 5.8 add_convert_fusion.1
  496.6 2.9 multiply_reduce_fusion.1
  499.5 1.4 multiply_add_fusion
  501.0 0.1 copy-done.40
  501.1 1.9 fusion.64
  503.0 1.6 fusion.75
  504.6 30.4 %multiply_reduce_fusion = (f32[6,128]{1,0:T(8,128)S(1)}, f32[6,128,4096]{2,1,0:T(8,128)}) fusion(f32[6,128,4096]{2,1,0:T(8,128)} %get-tuple-element.31, f32[6,128]{1,0:T(8,128)S(1)} %log_add_fusion, bf16[6,128,1024]{2,1,0:T(8,128)(2,1)S(1)} %fusion.64, bf16[6,4096,1024]{2,1,0:T(8,128)(2,1)} %convolution_convert_fusion), kind=kOutput, calls=%fused_computation.5 | convolution fusion | flops 6451887104 | bytes 77076480 | tf_op jit(solution)/shard_map/bld,bmd->blm/dot_general | solution.py:114
  535.0 15.0 fusion.1
  550.0 13.4 fusion.26
  563.4 18.9 %add_convert_fusion = bf16[6,4096,261]{1,2,0:T(8,128)(2,1)} fusion(f32[6,4096,261]{1,2,0:T(8,128)} %fusion.26, bf16[6,128,4096]{2,1,0:T(8,128)(2,1)} %get-tuple-element.28, bf16[6,128,4096]{2,1,0:T(8,128)(2,1)} %get-tuple-element.29, f32[6,128,261]{1,2,0:T(8,128)} %fusion.75, f32[6,128,261]{1,2,0:T(8,128)S(1)} %copy-done.13), kind=kOutput, calls=%fused_computation.2 | convolution fusion | flops 3324139008 | bytes 52672512 | tf_op jit(solution)/shard_map/blm,blc->bmc/dot_general | solution.py:32
  582.4 11.8 fusion.25
  594.2 1.1 fusion.85
  595.3 0.1 copy-done.14
  595.4 2.2 bitcast_add_fusion
  597.7 2.3 fusion.84
  600.0 2.2 fusion.68
  602.3 6.4 convolution_bitcast_fusion.1
  608.7 1.8 copy-done.11
  610.6 5.2 convolution_bitcast_fusion.2
  615.9 20.0 %multiply_convert_fusion.1 = bf16[6,128,1024]{2,1,0:T(8,128)(2,1)S(1)} fusion(bf16[6,128,4096]{2,1,0:T(8,128)(2,1)} %get-tuple-element.29, bf16[6,4096,1024]{2,1,0:T(8,128)(2,1)} %convolution_convert_fusion.1), kind=kOutput, calls=%fused_computation.60 | convolution fusion | flops 6444023808 | bytes 58195968 | tf_op jit(solution)/shard_map/blm,bmd->bld/dot_general | solution.py:118
  635.9 4.0 convolution_bitcast_fusion.3
  640.0 5.8 convolution_bitcast_fusion
  645.8 4.1 fusion.33
  649.9 2.1 fusion.32
  652.1 0.7 copy-done.21
  652.8 0.7 copy-done.39
  653.5 3.0 add_convert_fusion.2
  656.5 143.1 %reduce-scatter.8.cloned.1.call-done = bf16[6,1024,261]{1,2,0:T(8,128)(2,1)} async-done(((bf16[6,4096,261]{1,2,0:T(8,128)(2,1)}), bf16[6,1024,261]{1,2,0:T(8,128)(2,1)}) %reduce-scatter.8.cloned.1.call-update) | async-done | bytes 3207184 | tf_op jit(solution)/shard_map/reduce_scatter | solution.py:131
  799.6 4.6 fusion.15
  804.2 41.8 %all-reduce = (f32[1024]{0:T(1024)}, f32[261]{0:T(512)}, f32[1024]{0:T(1024)}) all-reduce(f32[1024]{0:T(1024)S(1)} %get-tuple-element.16, f32[261]{0:T(512)S(1)} %get-tuple-element.12, f32[1024]{0:T(1024)S(1)} %copy-done.38), channel_id=1, replica_groups=mesh['img'=8,'lat'=4] {'img','lat'}, use_global_device_ids=true, to_apply=%region_23.24 | all-reduce | flops 2309 | bytes 18472 | tf_op jit(solution)/shard_map/psum | solution.py:148
  846.0 5.8 fusion.12
  851.7 52.6 %reduce-scatter.14.cloned.1.call-done = f32[261,32]{0,1:T(8,128)} async-done(((f32[261,1024]{0,1:T(8,128)}), f32[261,32]{0,1:T(8,128)}) %reduce-scatter.14.cloned.1.call-update) | async-done | bytes 33424 | tf_op jit(solution)/shard_map/reduce_scatter | solution.py:143
  904.3 102.8 %reduce-scatter.12.cloned.1.call-done = f32[261,32]{0,1:T(8,128)} async-done(((f32[261,1024]{0,1:T(8,128)}), f32[261,32]{0,1:T(8,128)}) %reduce-scatter.12.cloned.1.call-update) | async-done | bytes 33424 | tf_op jit(solution)/shard_map/reduce_scatter | solution.py:142
  1007.1 150.7 %reduce-scatter.18.cloned.1.call-done = f32[32,1024]{1,0:T(8,128)} async-done(((f32[1024,1024]{1,0:T(8,128)}), f32[32,1024]{1,0:T(8,128)}) %reduce-scatter.18.cloned.1.call-update) | async-done | bytes 131088 | tf_op jit(solution)/shard_map/reduce_scatter | solution.py:145
  1157.8 149.0 %reduce-scatter.16.cloned.1.call-done = f32[32,1024]{1,0:T(8,128)} async-done(((f32[1024,1024]{1,0:T(8,128)}), f32[32,1024]{1,0:T(8,128)}) %reduce-scatter.16.cloned.1.call-update) | async-done | bytes 131088 | tf_op jit(solution)/shard_map/reduce_scatter | solution.py:144
  1306.9 149.2 %reduce-scatter.10.cloned.1.call-done = f32[32,1024]{1,0:T(8,128)} async-done(((f32[1024,1024]{1,0:T(8,128)}), f32[32,1024]{1,0:T(8,128)}) %reduce-scatter.10.cloned.1.call-update) | async-done | bytes 131088 | tf_op jit(solution)/shard_map/reduce_scatter | solution.py:141
  1456.0 148.3 %reduce-scatter.20.cloned.1.call-done = f32[32,1024]{1,0:T(8,128)} async-done(((f32[1024,1024]{1,0:T(8,128)}), f32[32,1024]{1,0:T(8,128)}) %reduce-scatter.20.cloned.1.call-update) | async-done | bytes 131088 | tf_op jit(solution)/shard_map/reduce_scatter | solution.py:146
  (118 shorter events, 1.0 us)
Async XLA Ops:
  7.2 3.6 copy-start.2
  7.2 232.7 %all-gather.6.cloned.1.call-start = ((), (), s32[]{:S(2)}) async-start(), calls=%async_computation.7 | async-start | bytes 2162688 | tf_op jit(solution)/shard_map/all_gather | solution.py:53
  7.9 4.4 copy-start.31
  7.9 308.9 %all-gather.8.cloned.1.call-start = ((), (), s32[]{:S(2)}) async-start(), calls=%async_computation.8 | async-start | bytes 16220160 | tf_op jit(solution)/shard_map/all_gather | solution.py:67
  10.7 0.9 copy-start.22
  11.7 0.6 copy-start.24
  15.2 2.0 copy-start.4
  15.2 2.9 copy-start.28
  15.2 17.9 %copy-start.29 = (bf16[261,32]{0,1:T(8,128)(2,1)S(1)}, bf16[261,32]{0,1:T(8,128)(2,1)}, u32[]{:S(2)}) copy-start(bf16[261,32]{0,1:T(8,128)(2,1)} %param.21) | copy-start | bytes 50116
  15.2 106.4 %copy-start.30 = (bf16[261,32]{0,1:T(8,128)(2,1)S(1)}, bf16[261,32]{0,1:T(8,128)(2,1)}, u32[]{:S(2)}) copy-start(bf16[261,32]{0,1:T(8,128)(2,1)} %param.22) | copy-start | bytes 50116
  15.2 224.6 %copy-start.36 = (f32[1024]{0:T(1024)S(1)}, f32[1024]{0:T(1024)}, u32[]{:S(2)}) copy-start(f32[1024]{0:T(1024)} %param.17) | copy-start | bytes 12292
  15.3 424.3 %all-gather.10.cloned.1.call-start = ((), (), s32[]{:S(2)}) async-start(), calls=%async_computation.9 | async-start | bytes 2162688 | tf_op jit(solution)/shard_map/all_gather | solution.py:56
  16.0 429.7 %all-gather.12.cloned.1.call-start = ((), (), s32[]{:S(2)}) async-start(), calls=%async_computation.10 | async-start | bytes 2162688 | tf_op jit(solution)/shard_map/all_gather | solution.py:57
  16.6 474.2 %all-gather.14.cloned.1.call-start = ((), (), s32[]{:S(2)}) async-start(), calls=%async_computation.11 | async-start | bytes 2162688 | tf_op jit(solution)/shard_map/all_gather | solution.py:58
  17.2 782.4 %reduce-scatter.8.cloned.1.call-start = ((), (), s32[]{:S(2)}) async-start(), calls=%async_computation.12 | async-start | bytes 16220160 | tf_op jit(solution)/shard_map/reduce_scatter | solution.py:131
  17.5 225.9 %copy-start.26 = (f32[6,128]{1,0:T(8,128)}, f32[6,128]{1,0:T(8,128)S(1)}, u32[]{:S(2)}) copy-start(f32[6,128]{1,0:T(8,128)S(1)} %broadcast_multiply_fusion.8) | copy-start | bytes 9220
  18.1 225.3 %copy-start.33 = (f32[6,128]{1,0:T(8,128)}, f32[6,128]{1,0:T(8,128)S(1)}, u32[]{:S(2)}) copy-start(f32[6,128]{1,0:T(8,128)S(1)} %add_rsqrt_fusion.2) | copy-start | bytes 9220
  239.9 3.6 copy-start.18
  243.4 107.3 %copy-start = (bf16[6,128,1024]{2,1,0:T(8,128)(2,1)}, bf16[6,128,1024]{2,1,0:T(8,128)(2,1)S(1)}, u32[]{:S(2)}) copy-start(bf16[6,128,1024]{2,1,0:T(8,128)(2,1)S(1)} %fusion.61) | copy-start | bytes 4718596
  243.4 73.4 %copy-start.19 = (bf16[261,1024]{0,1:T(8,128)(2,1)S(1)}, bf16[261,1024]{0,1:T(8,128)(2,1)}, u32[]{:S(2)}) copy-start(bf16[261,1024]{0,1:T(8,128)(2,1)} %all_gather.33) | copy-start | bytes 1603588
  376.6 6.4 copy-start.16
  416.9 22.7 %copy-start.5 = (bf16[6,128,1024]{2,1,0:T(8,128)(2,1)S(1)}, bf16[6,128,1024]{2,1,0:T(8,128)(2,1)}, u32[]{:S(2)}) copy-start(bf16[6,128,1024]{2,1,0:T(8,128)(2,1)} %param.13) | copy-start | bytes 4718596
  439.5 4.1 copy-start.42
  443.6 1.7 copy-start.7
  443.6 2.2 copy-start.35
  490.8 5.8 copy-start.8
  490.8 5.8 copy-start.41
  496.6 2.9 copy-start.43
  496.6 2.9 copy-start.20
  499.5 1.6 copy-start.40
  501.1 1.9 copy-start.10
  501.1 1.9 copy-start.17
  535.0 15.0 copy-start.13
  582.4 322.0 %reduce-scatter.14.cloned.1.call-start = ((), (), s32[]{:S(2)}) async-start(), calls=%async_computation.15 | async-start | bytes 1622016 | tf_op jit(solution)/shard_map/reduce_scatter | solution.py:143
  594.2 1.2 copy-start.14
  595.4 2.3 copy-start.1
  597.6 2.4 copy-start.15
  597.6 409.5 %reduce-scatter.12.cloned.1.call-start = ((), (), s32[]{:S(2)}) async-start(), calls=%async_computation.14 | async-start | bytes 1622016 | tf_op jit(solution)/shard_map/reduce_scatter | solution.py:142
  602.2 555.6 %reduce-scatter.18.cloned.1.call-start = ((), (), s32[]{:S(2)}) async-start(), calls=%async_computation.17 | async-start | bytes 4325376 | tf_op jit(solution)/shard_map/reduce_scatter | solution.py:145
  608.7 1.9 copy-start.11
  608.7 698.2 %reduce-scatter.16.cloned.1.call-start = ((), (), s32[]{:S(2)}) async-start(), calls=%async_computation.16 | async-start | bytes 4325376 | tf_op jit(solution)/shard_map/reduce_scatter | solution.py:144
  615.8 20.1 %copy-start.6 = (bf16[6,128,1024]{2,1,0:T(8,128)(2,1)S(1)}, bf16[6,128,1024]{2,1,0:T(8,128)(2,1)}, u32[]{:S(2)}) copy-start(bf16[6,128,1024]{2,1,0:T(8,128)(2,1)} %param.13) | copy-start | bytes 4718596
  615.8 20.1 %copy-start.27 = (f32[6,128]{1,0:T(8,128)S(1)}, f32[6,128]{1,0:T(8,128)}, u32[]{:S(2)}) copy-start(f32[6,128]{1,0:T(8,128)} %copy-done.26) | copy-start | bytes 9220
  615.9 20.1 %copy-start.34 = (f32[6,128]{1,0:T(8,128)S(1)}, f32[6,128]{1,0:T(8,128)}, u32[]{:S(2)}) copy-start(f32[6,128]{1,0:T(8,128)} %copy-done.33) | copy-start | bytes 9220
  615.9 20.1 %copy-start.37 = (f32[1024]{0:T(1024)S(1)}, f32[1024]{0:T(1024)}, u32[]{:S(2)}) copy-start(f32[1024]{0:T(1024)} %param.17) | copy-start | bytes 12292
  615.9 840.1 %reduce-scatter.10.cloned.1.call-start = ((), (), s32[]{:S(2)}) async-start(), calls=%async_computation.13 | async-start | bytes 4325376 | tf_op jit(solution)/shard_map/reduce_scatter | solution.py:141
  640.0 964.4 %reduce-scatter.20.cloned.1.call-start = ((), (), s32[]{:S(2)}) async-start(), calls=%async_computation.18 | async-start | bytes 4325376 | tf_op jit(solution)/shard_map/reduce_scatter | solution.py:146
  645.8 4.1 copy-start.12
  649.9 2.2 copy-start.9
  649.9 2.9 copy-start.21
  649.9 3.6 copy-start.39
  653.5 146.1 %copy-start.3 = (bf16[6,1024,261]{1,2,0:T(8,128)(2,1)S(1)}, bf16[6,1024,261]{1,2,0:T(8,128)(2,1)}, u32[]{:S(2)}) copy-start(bf16[6,1024,261]{1,2,0:T(8,128)(2,1)} %param.14) | copy-start | bytes 9621508
  653.5 146.1 %copy-start.23 = (f32[6,1024]{1,0:T(8,128)S(1)}, f32[6,1024]{1,0:T(8,128)}, u32[]{:S(2)}) copy-start(f32[6,1024]{1,0:T(8,128)} %copy-done.22) | copy-start | bytes 73732
  653.5 146.1 %copy-start.25 = (f32[6,1024]{1,0:T(8,128)S(1)}, f32[6,1024]{1,0:T(8,128)}, u32[]{:S(2)}) copy-start(f32[6,1024]{1,0:T(8,128)} %copy-done.24) | copy-start | bytes 73732
  653.5 146.1 %copy-start.32 = (f32[261]{0:T(512)S(1)}, f32[261]{0:T(512)}, u32[]{:S(2)}) copy-start(f32[261]{0:T(512)} %param.18) | copy-start | bytes 3136
  656.5 147.6 %copy-start.38 = (f32[1024]{0:T(1024)S(1)}, f32[1024]{0:T(1024)}, u32[]{:S(2)}) copy-start(f32[1024]{0:T(1024)} %get-tuple-element.14) | copy-start | bytes 12292
Sparse Core Ops, SparseCore 0:
  10.9 59.5 all-gather.5
  72.7 244.1 all-gather.7
  319.8 54.6 all-gather.9
  377.3 55.3 all-gather.11
  435.4 55.3 all-gather.13
  582.5 217.0 reduce-scatter.7
  806.2 98.0 reduce-scatter.13
  911.0 96.0 reduce-scatter.11
  1010.1 147.7 reduce-scatter.17
  1160.6 146.1 reduce-scatter.15
  1309.8 146.1 reduce-scatter.9
  1458.8 145.4 reduce-scatter.19
where the time goes:
time: 1620 us; the launch traced here: 1610 us
  waiting for transfers between devices  1000 us (62%)
  matrix products  273 us (17%)
  blocking collectives  263 us (16%)
  other arithmetic  51.3 us (3%)
    reduce_scatter x1, waiting for transfers between devices, local(): lax.psum_scatter(grad_hidden, ('img', 'lat'), scatter_dimension=0, tiled=...  151 us
    reduce_scatter x1, waiting for transfers between devices, local(): lax.psum_scatter(grad_query, ('img', 'lat'), scatter_dimension=0, tiled=T...  149 us
    reduce_scatter x1, waiting for transfers between devices, local(): lax.psum_scatter(grad_output, ('img', 'lat'), scatter_dimension=0, tiled=...  149 us
    reduce_scatter x1, waiting for transfers between devices, local(): lax.psum_scatter(grad_return, ('img', 'lat'), scatter_dimension=0, tiled=...  148 us
    reduce_scatter x1, waiting for transfers between devices, local(): lax.psum_scatter(grad_pix_all.astype(jnp.bfloat16), 'lat', scatter_dimens...  143 us
    all_gather x1, blocking collectives, local(): lax.all_gather(w_value, ('img', 'lat'), axis=1, tiled=True)  118 us
    reduce_scatter x1, waiting for transfers between devices, local(): lax.psum_scatter(grad_key, ('img', 'lat'), scatter_dimension=1, tiled=True)  103 us
    all_gather x1, blocking collectives, local(): lax.all_gather(w_key, ('img', 'lat'), axis=1, tiled=True)  88.5 us
  transfers between devices with their start and end apart: 12, of which 9 were waited for; matrix products, arithmetic and copies ran while one was open for 14% of the time, Pallas kernels for 0%

commit v1 on v0

v1 whole, which is shorter than its diff:
```python
from functools import partial

import jax
import jax.numpy as jnp
from jax import lax
from jax.experimental import pallas as pl
from jax.experimental.pallas import tpu as pltpu
from jax.sharding import PartitionSpec as P

F32 = jnp.float32
BF16 = jnp.bfloat16
AXES = ("img", "lat")
OUT_OF_SIGHT = -1e30
VMEM = 56 * 1024 * 1024


def round_up(value, unit):
    return -(-value // unit) * unit


def normalize(values):
    centered = values - jnp.mean(values, -1, keepdims=True)
    rstd = lax.rsqrt(jnp.mean(centered * centered, -1, keepdims=True) + 1e-05)
    return (centered * rstd, rstd)


def norm_back(upstream, normed, rstd):
    return rstd * (
        upstream
        - jnp.mean(upstream, -1, keepdims=True)
        - normed * jnp.mean(upstream * normed, -1, keepdims=True)
    )


def dot(left, right, contract):
    return lax.dot_general(left, right, (contract, ((), ())), preferred_element_type=F32)


def img_bits(parts):
    return parts.bit_length() - 1


def swap_img(value, bit, parts):
    return lax.ppermute(value, "img", [(i, i ^ (1 << bit)) for i in range(parts)])


def bit_of(bit):
    return (lax.axis_index("img") >> bit) & 1


def ordered(own, other, bit, axis):
    is_low = bit_of(bit) == 0
    return jnp.concatenate(
        [jnp.where(is_low, own, other), jnp.where(is_low, other, own)], axis=axis
    )


def lat_blocks(value, size):
    blocks = [value]
    for step in range(1, size):
        pairs = [(i, i ^ step) for i in range(size)]
        blocks.append(lax.ppermute(value, "lat", pairs))
    return blocks


def lat_ordered(blocks):
    stacked = jnp.stack(blocks)
    me = lax.axis_index("lat")
    return jnp.concatenate(
        [lax.dynamic_index_in_dim(stacked, me ^ j, 0, False) for j in range(len(blocks))], axis=0
    )


def gather_rows(shard, imgs, lats):
    rows = lat_ordered(lat_blocks(shard, lats))
    span = rows.shape[0]
    for bit in reversed(range(img_bits(imgs))):
        other = swap_img(rows, bit, imgs)
        grouped = rows.reshape(-1, 1, span, rows.shape[-1])
        grouped_other = other.reshape(-1, 1, span, rows.shape[-1])
        rows = ordered(grouped, grouped_other, bit, 1).reshape(-1, rows.shape[-1])
    return rows


def scatter_rows(total, imgs, lats):
    columns = total.shape[-1]
    span = total.shape[0] // imgs
    for bit in range(img_bits(imgs)):
        halves = total.reshape(-1, 2, span, columns)
        is_low = bit_of(bit) == 0
        mine = jnp.where(is_low, halves[:, 0], halves[:, 1])
        sent = jnp.where(is_low, halves[:, 1], halves[:, 0]).astype(BF16)
        total = mine + swap_img(sent, bit, imgs).astype(F32)
    blocks = total.reshape(lats, span // lats, columns)
    me = lax.axis_index("lat")
    result = lax.dynamic_index_in_dim(blocks, me, 0, False)
    for step in range(1, lats):
        sent = lax.dynamic_index_in_dim(blocks, me ^ step, 0, False).astype(BF16)
        pairs = [(i, i ^ step) for i in range(lats)]
        result = result + lax.ppermute(sent, "lat", pairs).astype(F32)
    return result


def sum_everywhere(total, imgs, lats):
    for bit in range(img_bits(imgs)):
        half = total.shape[-1] // 2
        is_low = bit_of(bit) == 0
        mine = jnp.where(is_low, total[:, :half], total[:, half:])
        sent = jnp.where(is_low, total[:, half:], total[:, :half]).astype(BF16)
        total = mine + swap_img(sent, bit, imgs).astype(F32)
    terms = [block.astype(F32) for block in lat_blocks(total.astype(BF16), lats)]
    while len(terms) > 1:
        terms = [terms[i] + terms[i + 1] for i in range(0, len(terms), 2)]
    whole = terms[0].astype(BF16)
    for bit in reversed(range(img_bits(imgs))):
        whole = ordered(whole, swap_img(whole, bit, imgs), bit, 1)
    return whole


def lat_gather(value, size):
    return lat_blocks(value, size)


def lat_return(blocks, size):
    out = [blocks[0]]
    for step in range(1, size):
        pairs = [(i, i ^ step) for i in range(size)]
        out.append(lax.ppermute(blocks[step], "lat", pairs))
    return out


def pixel_kernel(channels, raw_ref, bias_ref, gain_ref, wide_ref, tall_ref, work):
    raw = raw_ref[0].astype(F32)
    rows = work.shape[0]
    centered = raw - jnp.sum(raw, 0, keepdims=True) * (1.0 / channels)
    rstd = lax.rsqrt(jnp.sum(centered * centered, 0, keepdims=True) * (1.0 / channels) + 1e-05)
    base = channels // 8 * 8
    row = lax.broadcasted_iota(jnp.int32, (rows - base, raw.shape[1]), 0) + base
    work[base:rows] = jnp.where((row > channels) & (row < channels + 6), 1.0, 0.0).astype(F32)
    work[0:channels] = centered * rstd * gain_ref[...]
    work[channels : channels + 1] = bias_ref[0]
    whole = work[...]
    wide_ref[0] = whole[: wide_ref.shape[1]].astype(BF16)
    tall_ref[0] = whole.T.astype(BF16)


def pixel_prep(raw, bias, gain, rows):
    images, channels, pixels = raw.shape
    lanes = round_up(rows, 128)
    return pl.pallas_call(
        partial(pixel_kernel, channels),
        grid=(images,),
        in_specs=[
            pl.BlockSpec((1, channels, pixels), lambda b: (b, 0, 0)),
            pl.BlockSpec((1, 1, pixels), lambda b: (b, 0, 0)),
            pl.BlockSpec((channels, 1), lambda b: (0, 0)),
        ],
        out_specs=[
            pl.BlockSpec((1, rows, pixels), lambda b: (b, 0, 0)),
            pl.BlockSpec((1, pixels, lanes), lambda b: (b, 0, 0)),
        ],
        out_shape=[
            jax.ShapeDtypeStruct((images, rows, pixels), BF16),
            jax.ShapeDtypeStruct((images, pixels, lanes), BF16),
        ],
        scratch_shapes=[pltpu.VMEM((lanes, pixels), F32)],
        compiler_params=pltpu.CompilerParams(vmem_limit_bytes=VMEM),
        cost_estimate=pl.CostEstimate(
            flops=images * channels * pixels * 10,
            bytes_accessed=images * pixels * (channels + rows + lanes) * 2,
            transcendentals=0,
        ),
    )(raw, bias, gain)


def split3(value):
    first = lax.reduce_precision(value, 8, 7)
    second = lax.reduce_precision(value - first, 8, 7)
    return (first.astype(BF16), second.astype(BF16), (value - first - second).astype(BF16))


def attend_kernel(channels, blocks, tile, *refs):
    wide_ref, tall_ref = refs[:2]
    query_refs = refs[2 : 2 + blocks]
    out_refs = refs[2 + blocks : 2 + 2 * blocks]
    weight, scores = refs[2 + 2 * blocks :]
    rows = wide_ref.shape[1]
    pixels = wide_ref.shape[2]
    span = query_refs[0].shape[2]
    weight[:rows] = jnp.concatenate([ref[0] for ref in query_refs], axis=1)
    weight[rows:] = jnp.zeros((weight.shape[0] - rows, weight.shape[1]), BF16)
    top = None
    for at in range(0, pixels, tile):
        part = dot(tall_ref[0, at : at + tile], weight[...], ((1,), (0,)))
        scores[at : at + tile] = part
        part_top = jnp.max(part, 0, keepdims=True)
        top = part_top if top is None else jnp.maximum(top, part_top)
    total = jnp.zeros((rows, weight.shape[1]), F32)
    for at in range(0, pixels, tile):
        expo = jnp.exp(scores[at : at + tile] - top).astype(BF16)
        total += dot(wide_ref[0, :, at : at + tile], expo, ((1,), (0,)))
    mass = total[channels + 1 : channels + 2]
    attended = total * (1.0 / mass)
    log_mass = top + jnp.log(mass)
    first = log_mass.astype(BF16).astype(F32)
    second = (log_mass - first).astype(BF16).astype(F32)
    parts = [first, second, log_mass - first - second]
    row = lax.broadcasted_iota(jnp.int32, total.shape, 0)
    attended = jnp.where(row < channels, attended, 0.0)
    for k, part in enumerate(parts):
        attended = jnp.where(row == channels + 1 + k, part, attended)
    attended = attended.astype(BF16)
    for k, ref in enumerate(out_refs):
        ref[0] = attended[:, k * span : (k + 1) * span]


def attend(wide, tall, queries, channels, span):
    images, rows, pixels = wide.shape
    lanes = tall.shape[2]
    blocks = len(queries)
    tile = min(256, pixels)
    block = pl.BlockSpec((1, rows, span), lambda b: (b, 0, 0))
    return pl.pallas_call(
        partial(attend_kernel, channels, blocks, tile),
        grid=(images,),
        in_specs=[
            pl.BlockSpec((1, rows, pixels), lambda b: (b, 0, 0)),
            pl.BlockSpec((1, pixels, lanes), lambda b: (b, 0, 0)),
        ]
        + [block] * blocks,
        out_specs=[block] * blocks,
        out_shape=[jax.ShapeDtypeStruct((images, rows, span), BF16)] * blocks,
        scratch_shapes=[
            pltpu.VMEM((lanes, blocks * span), BF16),
            pltpu.VMEM((pixels, blocks * span), F32),
        ],
        compiler_params=pltpu.CompilerParams(vmem_limit_bytes=VMEM),
        cost_estimate=pl.CostEstimate(
            flops=images * pixels * blocks * span * rows * 4,
            bytes_accessed=images * pixels * (rows + lanes) * 2 + images * rows * blocks * span * 4,
            transcendentals=images * pixels * blocks * span,
        ),
    )(wide, tall, *queries)


def attend_back_kernel(channels, blocks, tile, *refs):
    wide_ref, tall_ref, raw_ref, gain_ref = refs[:4]
    query_refs = refs[4 : 4 + blocks]
    att_refs = refs[4 + blocks : 4 + 2 * blocks]
    grad_ref = refs[4 + 2 * blocks]
    out_refs = refs[5 + 2 * blocks : 5 + 3 * blocks]
    query_weight, att_weight = refs[5 + 3 * blocks :]
    rows = wide_ref.shape[1]
    pixels = wide_ref.shape[2]
    span = query_refs[0].shape[2]
    width = blocks * span
    queries = jnp.concatenate([ref[0] for ref in query_refs], axis=1)
    atts = jnp.concatenate([ref[0] for ref in att_refs], axis=1)
    row = lax.broadcasted_iota(jnp.int32, (rows, width), 0)
    shifts = (row > channels) & (row < channels + 4)
    query_weight[:rows] = jnp.where(shifts, atts.astype(F32), queries.astype(F32)).astype(BF16)
    att_weight[:rows] = jnp.where(shifts, 0.0, atts.astype(F32)).astype(BF16)
    fill = jnp.zeros((query_weight.shape[0] - rows, width), BF16)
    query_weight[rows:] = fill
    att_weight[rows:] = fill
    total = jnp.zeros((rows, width), F32)
    for at in range(0, pixels, tile):
        tall = tall_ref[0, at : at + tile]
        probs = jnp.exp(dot(tall, query_weight[...], ((1,), (0,))))
        grad = probs * dot(tall, att_weight[...], ((1,), (0,)))
        grad_low = grad.astype(BF16)
        probs_low = probs.astype(BF16)
        total += dot(wide_ref[0, :, at : at + tile], grad_low, ((1,), (0,)))
        into = dot(query_weight[:rows], grad_low, ((1,), (1,)))
        into += dot(att_weight[:rows], probs_low, ((1,), (1,)))
        raw = raw_ref[0, :, at : at + tile].astype(F32)
        centered = raw - jnp.sum(raw, 0, keepdims=True) * (1.0 / channels)
        rstd = lax.rsqrt(
            jnp.sum(centered * centered, 0, keepdims=True) * (1.0 / channels) + 1e-05
        )
        hat = centered * rstd
        upstream = into[:channels] * gain_ref[...]
        mean = jnp.sum(upstream, 0, keepdims=True) * (1.0 / channels)
        along = jnp.sum(upstream * hat, 0, keepdims=True) * (1.0 / channels)
        grad_ref[0, :, at : at + tile] = (rstd * (upstream - mean - hat * along)).astype(BF16)
    total = total.astype(BF16)
    for k, ref in enumerate(out_refs):
        ref[0] = total[:, k * span : (k + 1) * span]


def attend_back(wide, tall, raw, gain, queries, atts, channels, span):
    images, rows, pixels = wide.shape
    lanes = tall.shape[2]
    blocks = len(queries)
    tile = min(256, pixels)
    block = pl.BlockSpec((1, rows, span), lambda b: (b, 0, 0))
    whole = pl.BlockSpec((1, channels, pixels), lambda b: (b, 0, 0))
    results = pl.pallas_call(
        partial(attend_back_kernel, channels, blocks, tile),
        grid=(images,),
        in_specs=[
            pl.BlockSpec((1, rows, pixels), lambda b: (b, 0, 0)),
            pl.BlockSpec((1, pixels, lanes), lambda b: (b, 0, 0)),
            whole,
            pl.BlockSpec((channels, 1), lambda b: (0, 0)),
        ]
        + [block] * (2 * blocks),
        out_specs=[whole] + [block] * blocks,
        out_shape=[jax.ShapeDtypeStruct((images, channels, pixels), BF16)]
        + [jax.ShapeDtypeStruct((images, rows, span), BF16)] * blocks,
        scratch_shapes=[
            pltpu.VMEM((lanes, blocks * span), BF16),
            pltpu.VMEM((lanes, blocks * span), BF16),
        ],
        compiler_params=pltpu.CompilerParams(vmem_limit_bytes=VMEM),
        cost_estimate=pl.CostEstimate(
            flops=images * pixels * blocks * span * rows * 10,
            bytes_accessed=images * pixels * (rows * 3 + lanes) * 2
            + images * rows * blocks * span * 6,
            transcendentals=images * pixels * blocks * span,
        ),
    )(wide, tall, raw, gain, *queries, *atts)
    return results[0], results[1:]


def local(
    imgs,
    lats,
    latents,
    pixels,
    keep_mask,
    cotangent,
    gain_latent,
    gain_pixel,
    gain_mlp,
    w_query,
    w_key,
    w_value,
    w_output,
    w_hidden,
    w_return,
):
    images, span, depth = latents.shape
    channels = pixels.shape[2]
    devices = imgs * lats
    share = depth // devices
    rows = round_up(channels + 6, 16)
    scale = depth ** (-0.5)
    count = images * span
    me = lax.axis_index("img") * lats + lax.axis_index("lat")

    raw = jnp.swapaxes(pixels, 1, 2)
    bias = jnp.where(keep_mask > 0, 0.0, OUT_OF_SIGHT).astype(F32)[:, None, :]
    gain_column = gain_pixel[:, None]
    wide, tall = pixel_prep(raw, bias, gain_column, rows)

    key_rows = gather_rows(w_key.T, imgs, lats)
    query_rows = gather_rows(w_query, imgs, lats)
    query_key = (dot(key_rows, query_rows, ((0,), (1,))) * scale).astype(BF16)
    value_out = dot(w_value, w_output, ((1,), (0,)))
    value_out = sum_everywhere(value_out, imgs, lats)
    hidden = gather_rows(w_hidden, imgs, lats)
    back = gather_rows(w_return, imgs, lats)
    query_columns = lax.all_to_all(
        w_query.reshape(share, devices, share), AXES, 1, 0, tiled=True
    ).reshape(depth, share)

    lat_f = latents.reshape(count, depth).astype(F32)
    cot = cotangent.reshape(count, depth)
    lat_hat, lat_rstd = normalize(lat_f)
    lat_in = (lat_hat * gain_latent).astype(BF16)
    query = jnp.einsum(
        "cd,bld->bcl", query_key, lat_in.reshape(images, span, depth), preferred_element_type=F32
    ).astype(BF16)
    ones = jnp.ones((images, 1, span), BF16)
    zeros = jnp.zeros((images, rows - channels - 1, span), BF16)
    query = jnp.concatenate([query, ones, zeros], axis=1)
    queries = lat_gather(query, lats)

    parts = attend(wide, tall, queries, channels, span)
    parts = [part.astype(F32) for part in lat_return(parts, lats)]
    logs = [
        part[:, channels + 1] + part[:, channels + 2] + part[:, channels + 3] for part in parts
    ]
    top = logs[0]
    for log in logs[1:]:
        top = jnp.maximum(top, log)
    shares = [jnp.exp(log - top) for log in logs]
    mass = sum(shares)
    log_mass = top + jnp.log(mass)
    pooled = sum(
        part[:, :channels] * (weight / mass)[:, None] for part, weight in zip(parts, shares)
    )
    pooled_low = pooled.astype(BF16)

    attended = jnp.einsum("bcl,cd->bld", pooled_low, value_out, preferred_element_type=F32)
    middle = lat_f + attended.reshape(count, depth)
    mid_hat, mid_rstd = normalize(middle)
    mlp_in = (mid_hat * gain_mlp).astype(BF16)
    pre = dot(mlp_in, hidden, ((1,), (0,)))
    act, gelu_back = jax.vjp(partial(jax.nn.gelu, approximate=False), pre)
    act_low = act.astype(BF16)
    output = (middle + dot(act_low, back, ((1,), (0,)))).astype(BF16)

    grad_return = dot(act_low, cot, ((0,), (0,)))
    shard_r = scatter_rows(grad_return, imgs, lats)
    grad_act = dot(cot, back, ((1,), (1,)))
    grad_pre = gelu_back(grad_act)[0].astype(BF16)
    grad_hidden = dot(mlp_in, grad_pre, ((0,), (0,)))
    shard_h = scatter_rows(grad_hidden, imgs, lats)
    grad_mlp_in = dot(grad_pre, hidden, ((1,), (1,)))
    grad_gain_mlp = jnp.sum(grad_mlp_in * mid_hat, 0, keepdims=True)
    grad_middle = cot.astype(F32) + norm_back(grad_mlp_in * gain_mlp, mid_hat, mid_rstd)
    grad_branch = grad_middle.astype(BF16)

    branch = grad_branch.reshape(images, span, depth)
    att = jnp.einsum("cd,bld->bcl", value_out, branch, preferred_element_type=F32).astype(BF16)
    inner = jnp.sum(att.astype(F32) * pooled, 1)
    log_rows = [part[:, None] for part in split3(-log_mass)]
    inner_rows = [part[:, None] for part in split3(-inner)[:2]]
    empty = jnp.zeros((images, 1, span), BF16)
    filler = jnp.zeros((images, rows - channels - 6, span), BF16)
    att = jnp.concatenate([att, empty, *log_rows, *inner_rows, filler], axis=1)
    atts = lat_gather(att, lats)

    pooled_grad = jnp.einsum("bcl,bld->cd", pooled_low, branch, preferred_element_type=F32)
    pooled_grad = jnp.concatenate([pooled_grad, grad_gain_mlp], axis=0)
    pooled_grad = sum_everywhere(pooled_grad, imgs, lats)
    sum_mlp = pooled_grad[channels].astype(F32)
    pooled_grad = pooled_grad[:channels]
    shard_o = dot(w_value, pooled_grad, ((0,), (0,)))
    shard_v = dot(pooled_grad, w_output, ((1,), (1,)))

    grad_raw, terms = attend_back(wide, tall, raw, gain_column, queries, atts, channels, span)
    terms = [term.astype(F32) for term in lat_return(terms, lats)]
    grad_query_key = sum(terms)[:, :channels].astype(BF16)
    grad_lat_in = jnp.einsum("bcl,cd->bld", grad_query_key, query_key, preferred_element_type=F32)
    grad_lat_in = grad_lat_in.reshape(count, depth)
    grad_latents = (
        grad_middle + norm_back(grad_lat_in * gain_latent, lat_hat, lat_rstd)
    ).astype(BF16)

    latent_grad = jnp.einsum(
        "bcl,bld->cd", grad_query_key, lat_in.reshape(images, span, depth),
        preferred_element_type=F32,
    )
    latent_grad = sum_everywhere(latent_grad, imgs, lats)
    mine = lax.dynamic_slice_in_dim(latent_grad, me * share, share, 1)
    shard_q = dot(mine, key_rows, ((0,), (1,))) * scale
    shard_k = dot(latent_grad, query_columns, ((1,), (0,))) * scale
    with_key = query_key.astype(F32) * latent_grad.astype(F32)
    with_value = value_out.astype(F32) * pooled_grad.astype(F32)
    sum_lat = jnp.sum(with_key, 0) / gain_latent
    sum_pix = jnp.sum(with_key + with_value, 1) / gain_pixel
    return (
        output.reshape(images, span, depth),
        grad_latents.reshape(images, span, depth),
        jnp.swapaxes(grad_raw, 1, 2),
        shard_q,
        shard_k,
        shard_v,
        shard_o,
        shard_h,
        shard_r,
        sum_lat,
        sum_pix,
        sum_mlp,
    )


def solution(mesh):
    in_specs = (
        P("img", "lat", None),
        P("img", "lat", None),
        P("img", "lat"),
        P("img", "lat", None),
        P(),
        P(),
        P(),
        P(("img", "lat"), None),
        P(None, ("img", "lat")),
        P(None, ("img", "lat")),
        P(("img", "lat"), None),
        P(("img", "lat"), None),
        P(("img", "lat"), None),
    )
    out_specs = (
        P("img", "lat", None),
        P("img", "lat", None),
        P("img", "lat", None),
        P(("img", "lat"), None),
        P(None, ("img", "lat")),
        P(None, ("img", "lat")),
        P(("img", "lat"), None),
        P(("img", "lat"), None),
        P(("img", "lat"), None),
        P(),
        P(),
        P(),
    )
    step = partial(local, mesh.shape["img"], mesh.shape["lat"])
    return jax.shard_map(step, mesh=mesh, in_specs=in_specs, out_specs=out_specs, check_vma=False)
```

time: 1620 us -> 423 us (0.26)
  waiting for transfers between devices: 1000 us -> 139 us
  blocking collectives: 263 us -> 0 us
  matrix products: 273 us -> 37.2 us
  starting transfers between devices: 0.48 us -> 111 us
  Pallas kernels: 0 us -> 38.7 us
  local copies, waits for them, and re-layouts: 5.92 us -> 29.7 us
    reduce_scatter x7 -> x0, waiting for transfers between devices: 896 us -> none  [the longest x1 151 us: local(): lax.psum_scatter(grad_hidden, ('img', 'lat'), scatter_dimension=0, tiled=...]
    dot_general x27 -> x18, matrix products: 273 us -> 37.2 us  [the longest x12 30.9 us: dot(): lax.dot_general(left, right, (contract, ((), ())), preferred_element_type...]
    all_gather x3 -> x0, blocking collectives: 222 us -> none  [the longest x1 118 us: local(): lax.all_gather(w_value, ('img', 'lat'), axis=1, tiled=True)]
    ppermute x0 -> x75, waiting for transfers between devices: none -> 139 us  [the longest x6 46.7 us: lat_return(): out.append(lax.ppermute(blocks[step], 'lat', pairs))]
    ppermute x0 -> x75, starting transfers between devices: none -> 107 us  [the longest x27 63 us: lat_blocks(): blocks.append(lax.ppermute(value, 'lat', pairs))]
    all_gather x5 -> x0, waiting for transfers between devices: 104 us -> none  [the longest x1 71.8 us: local(): lax.all_gather(pix_in, 'lat', axis=1, tiled=True)]
    psum x1 -> x0, blocking collectives: 41.8 us -> none  [local(): lax.psum((grad_gain_latent, grad_gain_pixel, grad_gain_mlp), ('img', 'lat'))]
    pallas_call x0 -> x3, Pallas kernels: none -> 38.7 us  [the longest x1 19.9 us: attend_back(): pl.pallas_call(partial(attend_back_kernel, channels, blocks, tile), grid=...]
  transfers between devices with their start and end apart: 12 -> 76, of which waited for: 9 -> 28; matrix products, arithmetic and copies ran while one was open for 14% -> 21% of each run, Pallas kernels for 0% -> 9%
where the time goes in v1:
time: 423 us; the launch traced here: 418 us
  waiting for transfers between devices  139 us (33%)
  starting transfers between devices  111 us (26%)
  other arithmetic  60.7 us (14%)
  Pallas kernels  38.7 us (9%)
  matrix products  37.2 us (9%)
  local copies, waits for them, and re-layouts  29.7 us (7%)
    ppermute x27, starting transfers between devices, lat_blocks(): blocks.append(lax.ppermute(value, 'lat', pairs))  63 us
    ppermute x6, waiting for transfers between devices, lat_return(): out.append(lax.ppermute(blocks[step], 'lat', pairs))  46.7 us
    ppermute x27, waiting for transfers between devices, lat_blocks(): blocks.append(lax.ppermute(value, 'lat', pairs))  44.4 us
    ppermute x36, waiting for transfers between devices, swap_img(): return lax.ppermute(value, 'img', [(i, i ^ 1 << bit) for i in range(parts)])  43.1 us
    dot_general x12, matrix products, dot(): lax.dot_general(left, right, (contract, ((), ())), preferred_element_type...  30.9 us
    ppermute x36, starting transfers between devices, swap_img(): return lax.ppermute(value, 'img', [(i, i ^ 1 << bit) for i in range(parts)])  27.4 us
    pallas_call x1, Pallas kernels, attend_back(): pl.pallas_call(partial(attend_back_kernel, channels, blocks, tile), grid=...  19.9 us
    select_n x19, other arithmetic, ordered(): jnp.where(is_low, own, other)  16.1 us
  transfers between devices with their start and end apart: 76, of which 28 were waited for; matrix products, arithmetic and copies ran while one was open for 21% of the time, Pallas kernels for 9%

profile of v1, /device:TPU:0, one launch (start us, length us, event | category | flops | bytes accessed | tf_op | source)
XLA Modules:
  0.0 418.4 jit_solution(17420240911651617621)
XLA Ops:
  0.7 4.1 collective-permute-start.1
  7.3 2.9 collective-permute-start.29
  12.1 3.5 all-to-all-start
  15.6 1.7 convert_reduce_fusion
  22.9 7.9 %shard_map.220 = (bf16[6,272,1024]{2,1,0:T(8,128)(2,1)}, bf16[6,1024,384]{2,1,0:T(8,128)(2,1)}) custom-call(bf16[6,261,1024]{2,1,0:T(8,128)(2,1)} %bitcast.487, f32[6,1,1024]{2,1,0:T(1,128)} %broadcast_in_dim.24.bias_ref, f32[261,1]{1,0:T(8,128)} %broadcast_in_dim.31.gain_ref.refs_3_), custom_call_target="tpu_custom_call" | custom-call | flops 16035840 | bytes 11268096 | tf_op jit(solution)/shard_map/pallas_call | solution.py:150
  30.8 2.7 collective-permute-start.28
  36.0 1.8 collective-permute-start.34
  40.3 2.3 collective-permute-start.8
  42.7 4.0 collective-permute-done.34
  56.0 1.8 reshape.812
  57.7 1.7 reshape.769
  69.3 2.0 collective-permute-start.20
  73.7 4.1 collective-permute-start.23
  80.1 2.0 collective-permute-start.37
  85.8 1.9 reshape.771
  93.2 11.6 %collective-permute-done.10 = bf16[256,1024]{1,0:T(8,128)(2,1)} collective-permute-done((bf16[256,1024]{1,0:T(8,128)(2,1)}, bf16[256,1024]{1,0:T(8,128)(2,1)}, u32[]{:S(2)}, u32[]{:S(2)}) %collective-permute-start.10) | collective-permute-done | bytes 524320 | tf_op jit(solution)/shard_map/ppermute | solution.py:44
  112.3 3.8 bitcast_select_fusion.9
  119.2 3.2 collective-permute-start.14
  125.7 8.2 %collective-permute-done.14.refs_5_.refs_7_ = bf16[6,272,128]{2,1,0:T(8,128)(2,1)} collective-permute-done((bf16[6,272,128]{2,1,0:T(8,128)(2,1)}, bf16[6,272,128]{2,1,0:T(8,128)(2,1)}, u32[]{:S(2)}, u32[]{:S(2)}) %collective-permute-start.14) | collective-permute-done | bytes 417824 | tf_op jit(solution)/shard_map/ppermute | solution.py:62
  134.0 23.9 %collective-permute-done.13.refs_4_.refs_6_ = bf16[6,272,128]{2,1,0:T(8,128)(2,1)} collective-permute-done((bf16[6,272,128]{2,1,0:T(8,128)(2,1)}, bf16[6,272,128]{2,1,0:T(8,128)(2,1)}, u32[]{:S(2)}, u32[]{:S(2)}) %collective-permute-start.13) | collective-permute-done | bytes 417824 | tf_op jit(solution)/shard_map/ppermute | solution.py:62
  157.8 11.0 %shard_map.221 = (bf16[6,272,128]{2,1,0:T(8,128)(2,1)}, bf16[6,272,128]{2,1,0:T(8,128)(2,1)}, bf16[6,272,128]{2,1,0:T(8,128)(2,1)}, bf16[6,272,128]{2,1,0:T(8,128)(2,1)}) custom-call(bf16[6,272,1024]{2,1,0:T(8,128)(2,1)} %get-tuple-element.23.refs_0_, bf16[6,1024,384]{2,1,0:T(8,128)(2,1)} %get-tuple-element.24.refs_1_, ...), custom_call_target="tpu_custom_call" | custom-call | flops 3422552064 | bytes 11403264 | tf_op jit(solution)/shard_map/pallas_call | solution.py:223
  168.9 2.9 collective-permute-start.16
  177.7 10.1 %collective-permute-done.15 = bf16[6,272,128]{2,1,0:T(8,128)(2,1)S(1)} collective-permute-done((bf16[6,272,128]{2,1,0:T(8,128)(2,1)}, bf16[6,272,128]{2,1,0:T(8,128)(2,1)S(1)}, u32[]{:S(2)}, u32[]{:S(2)}) %collective-permute-start.15) | collective-permute-done | bytes 417824 | tf_op jit(solution)/shard_map/ppermute | solution.py:128
  187.8 12.8 %collective-permute-done.16 = bf16[6,272,128]{2,1,0:T(8,128)(2,1)S(1)} collective-permute-done((bf16[6,272,128]{2,1,0:T(8,128)(2,1)}, bf16[6,272,128]{2,1,0:T(8,128)(2,1)S(1)}, u32[]{:S(2)}, u32[]{:S(2)}) %collective-permute-start.16) | collective-permute-done | bytes 417824 | tf_op jit(solution)/shard_map/ppermute | solution.py:128
  203.6 8.9 %fusion = (f32[768,1024]{1,0:T(8,128)S(1)}, f32[768,1024]{1,0:T(8,128)S(1)}) fusion(bf16[768,1024]{1,0:T(8,128)(2,1)S(1)} %bitcast.499, bf16[1024,1024]{1,0:T(8,128)(2,1)S(1)} %bitcast.489), kind=kOutput, calls=%fused_computation.2 | convolution fusion | flops 1659371520 | bytes 9961472 | tf_op jit(solution)/shard_map/dot_general | solution.py:36
  212.5 7.2 %fusion.3 = bf16[1024,768]{0,1:T(8,128)(2,1)S(1)} fusion(f32[768,1024]{1,0:T(8,128)S(1)} %get-tuple-element.136), kind=kLoop, calls=%fused_computation.5 | loop fusion | flops 51118080 | bytes 4718592 | tf_op jit(solution)/shard_map/convert_element_type | solution.py:402
  219.8 3.1 add_convert_fusion
  222.9 2.7 fusion.15
  225.5 1.8 fusion.116
  227.4 2.7 multiply_reduce_fusion
  230.1 2.6 fusion.114
  237.5 5.1 %concatenate.104.refs_8_ = bf16[6,272,128]{2,1,0:T(8,128)(2,1)} concatenate(bf16[6,261,128]{2,1,0:T(8,128)(2,1)} %get-tuple-element.138, bf16[6,1,128]{2,1,0:T(2,128)(2,1)S(1)} %broadcast_in_dim.28, bf16[6,1,128]{2,1,0:T(2,128)(2,1)S(1)} %get-tuple-element.132, bf16[6,1,128]{2,1,0:T(2,128)(2,1)S(1)} %get-tuple-element.131, bf16[6,1,128]{2,1,0:T(2,128)(2,1)S(1)} %get-tuple-element.42, ...), dimensions={1} | concatenate | bytes 835584 | tf_op jit(solution)/shard_map/concatenate | solution.py:423
  242.6 2.2 collective-permute-start.41
  244.9 6.9 %collective-permute-start.40 = (bf16[6,272,128]{2,1,0:T(8,128)(2,1)}, bf16[6,272,128]{2,1,0:T(8,128)(2,1)}, u32[]{:S(2)}, u32[]{:S(2)}) collective-permute-start(bf16[6,272,128]{2,1,0:T(8,128)(2,1)} %concatenate.104.refs_8_), channel_id=1, source_target_pairs={{0,2},{1,3},{2,0},{3,1},{4,6},{5,7},{6,4},{7,5},{8,10},{9,11},{10,... | collective-permute-start | bytes 1253384 | tf_op jit(solution)/shard_map/ppermute | solution.py:62
  251.7 2.6 copy.199
  256.8 1.7 collective-permute-start.56
  258.5 5.7 %fusion.47 = f32[4,2,128,1024]{3,2,1,0:T(8,128)} fusion(bf16[4,2,128,768]{3,2,1,0:T(8,128)(2,1)} %bitcast.497, bf16[768,1024]{1,0:T(8,128)(2,1)} %copy-done.65), kind=kOutput, calls=%fused_computation.92 | convolution fusion | flops 1610612736 | bytes 7340032 | tf_op jit(solution)/shard_map/dot_general | solution.py:36
  264.3 1.7 copy.200
  267.0 2.0 collective-permute-start.59
  268.9 3.8 fusion.49
  272.8 1.7 collective-permute-start.58
  275.8 12.3 %collective-permute-start.57 = (bf16[262,128]{1,0:T(8,128)(2,1)S(1)}, bf16[262,128]{1,0:T(8,128)(2,1)S(1)}, u32[]{:S(2)}, u32[]{:S(2)}) collective-permute-start(bf16[262,128]{1,0:T(8,128)(2,1)S(1)} %add_convert_fusion.3), channel_id=1, source_target_pairs={{0,1},{1,0},{2,3},{3,2},{4,5},{5,4},{6,7},{7,6},{8,9},{9,8},{10,11... | collective-permute-start | bytes 201224 | tf_op jit(solution)/shard_map/ppermute | solution.py:62
  290.4 1.7 collective-permute-start.60
  292.2 19.9 %shard_map.222 = (bf16[6,261,1024]{2,1,0:T(8,128)(2,1)}, bf16[6,272,128]{2,1,0:T(8,128)(2,1)}, bf16[6,272,128]{2,1,0:T(8,128)(2,1)}, bf16[6,272,128]{2,1,0:T(8,128)(2,1)}, bf16[6,272,128]{2,1,0:T(8,128)(2,1)}) custom-call(bf16[6,272,1024]{2,1,0:T(8,128)(2,1)} %get-tuple-element.23.refs_0_, bf16[6,1024,384]{2,1,0:T(8,128)(2,1)} %get-tuple-element.24.refs_1_, ...), custom_call_target="tpu_custom_call" | custom-call | flops 8556380160 | bytes 19759104 | tf_op jit(solution)/shard_map/pallas_call | solution.py:298
  312.1 2.1 collective-permute-start.42
  314.7 1.9 collective-permute-start.44
  318.0 3.8 collective-permute-done.61
  321.9 8.1 %collective-permute-done.42 = bf16[6,272,128]{2,1,0:T(8,128)(2,1)S(1)} collective-permute-done((bf16[6,272,128]{2,1,0:T(8,128)(2,1)}, bf16[6,272,128]{2,1,0:T(8,128)(2,1)S(1)}, u32[]{:S(2)}, u32[]{:S(2)}) %collective-permute-start.42) | collective-permute-done | bytes 417824 | tf_op jit(solution)/shard_map/ppermute | solution.py:128
  329.9 15.8 %collective-permute-done.43 = bf16[6,272,128]{2,1,0:T(8,128)(2,1)S(1)} collective-permute-done((bf16[6,272,128]{2,1,0:T(8,128)(2,1)}, bf16[6,272,128]{2,1,0:T(8,128)(2,1)S(1)}, u32[]{:S(2)}, u32[]{:S(2)}) %collective-permute-start.43) | collective-permute-done | bytes 417824 | tf_op jit(solution)/shard_map/ppermute | solution.py:128
  348.7 2.3 fusion.9
  353.1 4.1 collective-permute-done.46
  357.6 2.0 fusion.45
  359.6 1.9 collective-permute-done.47
  361.6 2.0 collective-permute-start.50
  363.6 6.3 %collective-permute-start.49 = (bf16[261,128]{1,0:T(8,128)(2,1)S(1)}, bf16[261,128]{1,0:T(8,128)(2,1)S(1)}, u32[]{:S(2)}, u32[]{:S(2)}) collective-permute-start(bf16[261,128]{1,0:T(8,128)(2,1)S(1)} %add_convert_fusion.5), channel_id=1, source_target_pairs={{0,2},{1,3},{2,0},{3,1},{4,6},{5,7},{6,4},{7,5},{8,10},{9,11},{10,... | collective-permute-start | bytes 200456 | tf_op jit(solution)/shard_map/ppermute | solution.py:62
  371.1 1.8 collective-permute-done.49
  375.3 3.3 collective-permute-done.51
  380.9 6.9 %collective-permute-done.52 = bf16[261,256]{1,0:T(8,128)(2,1)S(1)} collective-permute-done((bf16[261,256]{1,0:T(8,128)(2,1)S(1)}, bf16[261,256]{1,0:T(8,128)(2,1)S(1)}, u32[]{:S(2)}, u32[]{:S(2)}) %collective-permute-start.52) | collective-permute-done | bytes 133664 | tf_op jit(solution)/shard_map/ppermute | solution.py:44
  388.7 7.1 %collective-permute-done.70 = bf16[2,128,1024]{2,1,0:T(8,128)(2,1)S(1)} collective-permute-done((bf16[2,128,1024]{2,1,0:T(8,128)(2,1)S(1)}, bf16[2,128,1024]{2,1,0:T(8,128)(2,1)S(1)}, u32[]{:S(2)}, u32[]{:S(2)}) %collective-permute-start.70) | collective-permute-done | bytes 524320 | tf_op jit(solution)/shard_map/ppermute | solution.py:44
  397.6 2.1 collective-permute-start.66
  399.7 1.9 collective-permute-start.68
  402.9 2.1 collective-permute-start.72
  404.9 1.9 collective-permute-start.74
  413.0 4.4 %collective-permute-done.73 = bf16[32,1024]{1,0:T(8,128)(2,1)S(1)} collective-permute-done((bf16[32,1024]{1,0:T(8,128)(2,1)S(1)}, bf16[32,1024]{1,0:T(8,128)(2,1)S(1)}, u32[]{:S(2)}, u32[]{:S(2)}) %collective-permute-start.73) | collective-permute-done | bytes 65568 | tf_op jit(solution)/shard_map/ppermute | solution.py:100
  (399 shorter events, 105.9 us)
Async XLA Ops:
  0.7 30.0 %collective-permute-start.1 = (bf16[32,261]{1,0:T(8,128)(2,1)}, bf16[32,261]{1,0:T(8,128)(2,1)S(1)}, u32[]{:S(2)}, u32[]{:S(2)}) collective-permute-start(bf16[32,261]{1,0:T(8,128)(2,1)} %bitcast.526), channel_id=1, source_target_pairs={{0,2},{1,3},{2,0},{3,1},{4,6},{5,7},{6,4},{7,5},{8,10},{9,11},{10,... | collective-permute-start | bytes 50120 | tf_op jit(solution)/shard_map/ppermute | solution.py:62
  4.8 28.6 %collective-permute-start = (bf16[32,261]{1,0:T(8,128)(2,1)}, bf16[32,261]{1,0:T(8,128)(2,1)S(1)}, u32[]{:S(2)}, u32[]{:S(2)}) collective-permute-start(bf16[32,261]{1,0:T(8,128)(2,1)} %bitcast.527), channel_id=1, source_target_pairs={{0,1},{1,0},{2,3},{3,2},{4,5},{5,4},{6,7},{7,6},{8,9},{9,8},{10,11... | collective-permute-start | bytes 50120 | tf_op jit(solution)/shard_map/ppermute | solution.py:62
  6.4 28.6 %collective-permute-start.2 = (bf16[32,261]{1,0:T(8,128)(2,1)}, bf16[32,261]{1,0:T(8,128)(2,1)S(1)}, u32[]{:S(2)}, u32[]{:S(2)}) collective-permute-start(bf16[32,261]{1,0:T(8,128)(2,1)} %bitcast.528), channel_id=1, source_target_pairs={{0,3},{1,2},{2,1},{3,0},{4,7},{5,6},{6,5},{7,4},{8,11},{9,10},{10,... | collective-permute-start | bytes 50120 | tf_op jit(solution)/shard_map/ppermute | solution.py:62
  6.4 29.6 %collective-permute-start.27 = (bf16[32,1024]{1,0:T(8,128)(2,1)}, bf16[32,1024]{1,0:T(8,128)(2,1)S(1)}, u32[]{:S(2)}, u32[]{:S(2)}) collective-permute-start(bf16[32,1024]{1,0:T(8,128)(2,1)} %param.24), channel_id=1, source_target_pairs={{0,1},{1,0},{2,3},{3,2},{4,5},{5,4},{6,7},{7,6},{8,9},{9,8},{10,11... | collective-permute-start | bytes 196616 | tf_op jit(solution)/shard_map/ppermute | solution.py:62
  7.3 30.4 %collective-permute-start.29 = (bf16[32,1024]{1,0:T(8,128)(2,1)}, bf16[32,1024]{1,0:T(8,128)(2,1)S(1)}, u32[]{:S(2)}, u32[]{:S(2)}) collective-permute-start(bf16[32,1024]{1,0:T(8,128)(2,1)} %param.24), channel_id=1, source_target_pairs={{0,3},{1,2},{2,1},{3,0},{4,7},{5,6},{6,5},{7,4},{8,11},{9,10},{10,... | collective-permute-start | bytes 196616 | tf_op jit(solution)/shard_map/ppermute | solution.py:62
  12.1 43.9 %all-to-all-start = ((bf16[32,2,512]{2,1,0:T(2,128)(2,1)}), bf16[32,2,512]{2,1,0:T(2,128)(2,1)}, u32[]{:S(2)}, u32[]{:S(2)}) async-start(bf16[32,2,512]{2,1,0:T(2,128)(2,1)} %reshape.811), calls=%async_computation | async-start | bytes 131072 | tf_op jit(solution)/shard_map/all_to_all | solution.py:364
  30.8 8.2 %collective-permute-start.28 = (bf16[32,1024]{1,0:T(8,128)(2,1)S(1)}, bf16[32,1024]{1,0:T(8,128)(2,1)S(1)}, u32[]{:S(2)}, u32[]{:S(2)}) collective-permute-start(bf16[32,1024]{1,0:T(8,128)(2,1)S(1)} %copy-done.48), channel_id=1, source_target_pairs={{0,2},{1,3},{2,0},{3,1},{4,6},{5,7},{6,4},{7,5},{8,10},{9,11},{10,... | collective-permute-start | bytes 196616 | tf_op jit(solution)/shard_map/ppermute | solution.py:62
  33.4 6.9 %collective-permute-start.33 = (bf16[32,1024]{1,0:T(8,128)(2,1)S(1)}, bf16[32,1024]{1,0:T(8,128)(2,1)S(1)}, u32[]{:S(2)}, u32[]{:S(2)}) collective-permute-start(bf16[32,1024]{1,0:T(8,128)(2,1)S(1)} %copy-done.49), channel_id=1, source_target_pairs={{0,1},{1,0},{2,3},{3,2},{4,5},{5,4},{6,7},{7,6},{8,9},{9,8},{10,11... | collective-permute-start | bytes 196616 | tf_op jit(solution)/shard_map/ppermute | solution.py:62
  35.0 7.7 %collective-permute-start.35 = (bf16[32,1024]{1,0:T(8,128)(2,1)S(1)}, bf16[32,1024]{1,0:T(8,128)(2,1)}, u32[]{:S(2)}, u32[]{:S(2)}) collective-permute-start(bf16[32,1024]{1,0:T(8,128)(2,1)S(1)} %copy-done.49), channel_id=1, source_target_pairs={{0,3},{1,2},{2,1},{3,0},{4,7},{5,6},{6,5},{7,4},{8,11},{9,10},{10,... | collective-permute-start | bytes 196616 | tf_op jit(solution)/shard_map/ppermute | solution.py:62
  36.0 10.7 %collective-permute-start.34 = (bf16[32,1024]{1,0:T(8,128)(2,1)S(1)}, bf16[32,1024]{1,0:T(8,128)(2,1)S(1)}, u32[]{:S(2)}, u32[]{:S(2)}) collective-permute-start(bf16[32,1024]{1,0:T(8,128)(2,1)S(1)} %copy-done.49), channel_id=1, source_target_pairs={{0,2},{1,3},{2,0},{3,1},{4,6},{5,7},{6,4},{7,5},{8,10},{9,11},{10,... | collective-permute-start | bytes 196616 | tf_op jit(solution)/shard_map/ppermute | solution.py:62
  37.7 11.2 %collective-permute-start.7 = (bf16[32,1024]{1,0:T(8,128)(2,1)S(1)}, bf16[32,1024]{1,0:T(8,128)(2,1)S(1)}, u32[]{:S(2)}, u32[]{:S(2)}) collective-permute-start(bf16[32,1024]{1,0:T(8,128)(2,1)S(1)} %copy-done.44), channel_id=1, source_target_pairs={{0,2},{1,3},{2,0},{3,1},{4,6},{5,7},{6,4},{7,5},{8,10},{9,11},{10,... | collective-permute-start | bytes 196616 | tf_op jit(solution)/shard_map/ppermute | solution.py:62
  39.0 11.4 %collective-permute-start.6 = (bf16[32,1024]{1,0:T(8,128)(2,1)S(1)}, bf16[32,1024]{1,0:T(8,128)(2,1)S(1)}, u32[]{:S(2)}, u32[]{:S(2)}) collective-permute-start(bf16[32,1024]{1,0:T(8,128)(2,1)S(1)} %copy-done.44), channel_id=1, source_target_pairs={{0,1},{1,0},{2,3},{3,2},{4,5},{5,4},{6,7},{7,6},{8,9},{9,8},{10,11... | collective-permute-start | bytes 196616 | tf_op jit(solution)/shard_map/ppermute | solution.py:62
  40.3 10.1 %collective-permute-start.8 = (bf16[32,1024]{1,0:T(8,128)(2,1)S(1)}, bf16[32,1024]{1,0:T(8,128)(2,1)S(1)}, u32[]{:S(2)}, u32[]{:S(2)}) collective-permute-start(bf16[32,1024]{1,0:T(8,128)(2,1)S(1)} %copy-done.44), channel_id=1, source_target_pairs={{0,3},{1,2},{2,1},{3,0},{4,7},{5,6},{6,5},{7,4},{8,11},{9,10},{10,... | collective-permute-start | bytes 196616 | tf_op jit(solution)/shard_map/ppermute | solution.py:62
  42.7 19.4 %collective-permute-start.18 = (bf16[261,512]{1,0:T(8,128)(2,1)}, bf16[261,512]{1,0:T(8,128)(2,1)}, u32[]{:S(2)}, u32[]{:S(2)}) collective-permute-start(bf16[261,512]{1,0:T(8,128)(2,1)} %select_convert_fusion.5), channel_id=1, source_target_pairs={{0,4},{4,0},{8,12},{12,8},{16,20},{20,16},{24,28},{28,24},{1,5},{5... | collective-permute-start | bytes 801800 | tf_op jit(solution)/shard_map/ppermute | solution.py:44
  48.9 15.9 %collective-permute-start.30 = (bf16[128,1024]{1,0:T(8,128)(2,1)}, bf16[128,1024]{1,0:T(8,128)(2,1)}, u32[]{:S(2)}, u32[]{:S(2)}) collective-permute-start(bf16[128,1024]{1,0:T(8,128)(2,1)} %pad_maximum_fusion.20), channel_id=1, source_target_pairs={{0,16},{4,20},{8,24},{12,28},{16,0},{20,4},{24,8},{28,12},{1,17},{... | collective-permute-start | bytes 786440 | tf_op jit(solution)/shard_map/ppermute | solution.py:44
  51.9 5.9 %collective-permute-start.4 = (bf16[256,261]{0,1:T(8,128)(2,1)}, bf16[256,261]{0,1:T(8,128)(2,1)}, u32[]{:S(2)}, u32[]{:S(2)}) collective-permute-start(bf16[256,261]{0,1:T(8,128)(2,1)} %bitcast.159), channel_id=1, source_target_pairs={{0,8},{4,12},{8,0},{12,4},{16,24},{20,28},{24,16},{28,20},{1,9},{5... | collective-permute-start | bytes 400904 | tf_op jit(solution)/shard_map/ppermute | solution.py:44
  53.2 14.1 %collective-permute-start.36 = (bf16[128,1024]{1,0:T(8,128)(2,1)}, bf16[128,1024]{1,0:T(8,128)(2,1)}, u32[]{:S(2)}, u32[]{:S(2)}) collective-permute-start(bf16[128,1024]{1,0:T(8,128)(2,1)} %pad_maximum_fusion.22), channel_id=1, source_target_pairs={{0,16},{4,20},{8,24},{12,28},{16,0},{20,4},{24,8},{28,12},{1,17},{... | collective-permute-start | bytes 786440 | tf_op jit(solution)/shard_map/ppermute | solution.py:44
  55.4 15.9 %collective-permute-start.9 = (bf16[128,1024]{1,0:T(8,128)(2,1)}, bf16[128,1024]{1,0:T(8,128)(2,1)}, u32[]{:S(2)}, u32[]{:S(2)}) collective-permute-start(bf16[128,1024]{1,0:T(8,128)(2,1)} %pad_maximum_fusion.18), channel_id=1, source_target_pairs={{0,16},{4,20},{8,24},{12,28},{16,0},{20,4},{24,8},{28,12},{1,17},{... | collective-permute-start | bytes 786440 | tf_op jit(solution)/shard_map/ppermute | solution.py:44
  62.0 23.9 %collective-permute-start.5 = (bf16[512,261]{0,1:T(8,128)(2,1)}, bf16[512,261]{0,1:T(8,128)(2,1)}, u32[]{:S(2)}, u32[]{:S(2)}) collective-permute-start(bf16[512,261]{0,1:T(8,128)(2,1)} %reshape.770), channel_id=1, source_target_pairs={{0,4},{4,0},{8,12},{12,8},{16,20},{20,16},{24,28},{28,24},{1,5},{5... | collective-permute-start | bytes 801800 | tf_op jit(solution)/shard_map/ppermute | solution.py:44
  63.3 5.9 %collective-permute-start.19 = (bf16[261,256]{1,0:T(8,128)(2,1)S(1)}, bf16[261,256]{1,0:T(8,128)(2,1)S(1)}, u32[]{:S(2)}, u32[]{:S(2)}) collective-permute-start(bf16[261,256]{1,0:T(8,128)(2,1)S(1)} %select_convert_fusion.10), channel_id=1, source_target_pairs={{0,8},{4,12},{8,0},{12,4},{16,24},{20,28},{24,16},{28,20},{1,9},{5... | collective-permute-start | bytes 400904 | tf_op jit(solution)/shard_map/ppermute | solution.py:44
  66.7 24.2 %collective-permute-start.31 = (bf16[256,1024]{1,0:T(8,128)(2,1)}, bf16[256,1024]{1,0:T(8,128)(2,1)}, u32[]{:S(2)}, u32[]{:S(2)}) collective-permute-start(bf16[256,1024]{1,0:T(8,128)(2,1)} %bitcast.49), channel_id=1, source_target_pairs={{0,8},{4,12},{8,0},{12,4},{16,24},{20,28},{24,16},{28,20},{1,9},{5... | collective-permute-start | bytes 1572872 | tf_op jit(solution)/shard_map/ppermute | solution.py:44
  73.7 6.4 %collective-permute-start.23 = (bf16[261,128]{1,0:T(8,128)(2,1)S(1)}, bf16[261,128]{1,0:T(8,128)(2,1)S(1)}, u32[]{:S(2)}, u32[]{:S(2)}) collective-permute-start(bf16[261,128]{1,0:T(8,128)(2,1)S(1)} %add_convert_fusion.7), channel_id=1, source_target_pairs={{0,3},{1,2},{2,1},{3,0},{4,7},{5,6},{6,5},{7,4},{8,11},{9,10},{10,... | collective-permute-start | bytes 200456 | tf_op jit(solution)/shard_map/ppermute | solution.py:62
  80.1 30.3 %collective-permute-start.37 = (bf16[256,1024]{1,0:T(8,128)(2,1)}, bf16[256,1024]{1,0:T(8,128)(2,1)}, u32[]{:S(2)}, u32[]{:S(2)}) collective-permute-start(bf16[256,1024]{1,0:T(8,128)(2,1)} %bitcast.67), channel_id=1, source_target_pairs={{0,8},{4,12},{8,0},{12,4},{16,24},{20,28},{24,16},{28,20},{1,9},{5... | collective-permute-start | bytes 1572872 | tf_op jit(solution)/shard_map/ppermute | solution.py:44
  85.4 19.4 %collective-permute-start.10 = (bf16[256,1024]{1,0:T(8,128)(2,1)}, bf16[256,1024]{1,0:T(8,128)(2,1)}, u32[]{:S(2)}, u32[]{:S(2)}) collective-permute-start(bf16[256,1024]{1,0:T(8,128)(2,1)} %bitcast.26), channel_id=1, source_target_pairs={{0,8},{4,12},{8,0},{12,4},{16,24},{20,28},{24,16},{28,20},{1,9},{5... | collective-permute-start | bytes 1572872 | tf_op jit(solution)/shard_map/ppermute | solution.py:44
  89.3 19.1 %collective-permute-start.25 = (bf16[261,256]{1,0:T(8,128)(2,1)}, bf16[261,256]{1,0:T(8,128)(2,1)}, u32[]{:S(2)}, u32[]{:S(2)}) collective-permute-start(bf16[261,256]{1,0:T(8,128)(2,1)} %pad_maximum_fusion.27), channel_id=1, source_target_pairs={{0,8},{4,12},{8,0},{12,4},{16,24},{20,28},{24,16},{28,20},{1,9},{5... | collective-permute-start | bytes 400904 | tf_op jit(solution)/shard_map/ppermute | solution.py:44
  107.1 5.2 %collective-permute-start.11 = (bf16[512,1024]{1,0:T(8,128)(2,1)}, bf16[512,1024]{1,0:T(8,128)(2,1)}, u32[]{:S(2)}, u32[]{:S(2)}) collective-permute-start(bf16[512,1024]{1,0:T(8,128)(2,1)} %bitcast.29), channel_id=1, source_target_pairs={{0,4},{4,0},{8,12},{12,8},{16,20},{20,16},{24,28},{28,24},{1,5},{5... | collective-permute-start | bytes 3145736 | tf_op jit(solution)/shard_map/ppermute | solution.py:44
  107.1 5.2 %collective-permute-start.32 = (bf16[512,1024]{1,0:T(8,128)(2,1)}, bf16[512,1024]{1,0:T(8,128)(2,1)}, u32[]{:S(2)}, u32[]{:S(2)}) collective-permute-start(bf16[512,1024]{1,0:T(8,128)(2,1)} %bitcast.53), channel_id=1, source_target_pairs={{0,4},{4,0},{8,12},{12,8},{16,20},{20,16},{24,28},{28,24},{1,5},{5... | collective-permute-start | bytes 3145736 | tf_op jit(solution)/shard_map/ppermute | solution.py:44
  110.5 14.2 %collective-permute-start.26 = (bf16[261,512]{1,0:T(8,128)(2,1)}, bf16[261,512]{1,0:T(8,128)(2,1)}, u32[]{:S(2)}, u32[]{:S(2)}) collective-permute-start(bf16[261,512]{1,0:T(8,128)(2,1)} %pad_maximum_fusion.14), channel_id=1, source_target_pairs={{0,4},{4,0},{8,12},{12,8},{16,20},{20,16},{24,28},{28,24},{1,5},{5... | collective-permute-start | bytes 801800 | tf_op jit(solution)/shard_map/ppermute | solution.py:44
  111.7 61.6 %collective-permute-start.38 = (bf16[512,1024]{1,0:T(8,128)(2,1)S(1)}, bf16[512,1024]{1,0:T(8,128)(2,1)}, u32[]{:S(2)}, u32[]{:S(2)}) collective-permute-start(bf16[512,1024]{1,0:T(8,128)(2,1)S(1)} %bitcast.486), channel_id=1, source_target_pairs={{0,4},{4,0},{8,12},{12,8},{16,20},{20,16},{24,28},{28,24},{1,5},{5... | collective-permute-start | bytes 3145736 | tf_op jit(solution)/shard_map/ppermute | solution.py:44
  119.2 14.8 %collective-permute-start.14 = (bf16[6,272,128]{2,1,0:T(8,128)(2,1)}, bf16[6,272,128]{2,1,0:T(8,128)(2,1)}, u32[]{:S(2)}, u32[]{:S(2)}) collective-permute-start(bf16[6,272,128]{2,1,0:T(8,128)(2,1)} %maximum_maximum_fusion.refs_2_.refs_4_), channel_id=1, source_target_pairs={{0,3},{1,2},{2,1},{3,0},{4,7},{5,6},{6,5},{7,4},{8,11},{9,10},{10,... | collective-permute-start | bytes 1253384 | tf_op jit(solution)/shard_map/ppermute | solution.py:62
  122.4 35.4 %collective-permute-start.13 = (bf16[6,272,128]{2,1,0:T(8,128)(2,1)}, bf16[6,272,128]{2,1,0:T(8,128)(2,1)}, u32[]{:S(2)}, u32[]{:S(2)}) collective-permute-start(bf16[6,272,128]{2,1,0:T(8,128)(2,1)} %maximum_maximum_fusion.refs_2_.refs_4_), channel_id=1, source_target_pairs={{0,2},{1,3},{2,0},{3,1},{4,6},{5,7},{6,4},{7,5},{8,10},{9,11},{10,... | collective-permute-start | bytes 1253384 | tf_op jit(solution)/shard_map/ppermute | solution.py:62
  122.4 35.4 %collective-permute-start.12 = (bf16[6,272,128]{2,1,0:T(8,128)(2,1)}, bf16[6,272,128]{2,1,0:T(8,128)(2,1)}, u32[]{:S(2)}, u32[]{:S(2)}) collective-permute-start(bf16[6,272,128]{2,1,0:T(8,128)(2,1)} %maximum_maximum_fusion.refs_2_.refs_4_), channel_id=1, source_target_pairs={{0,1},{1,0},{2,3},{3,2},{4,5},{5,4},{6,7},{7,6},{8,9},{9,8},{10,11... | collective-permute-start | bytes 1253384 | tf_op jit(solution)/shard_map/ppermute | solution.py:62
  168.8 18.9 %collective-permute-start.15 = (bf16[6,272,128]{2,1,0:T(8,128)(2,1)}, bf16[6,272,128]{2,1,0:T(8,128)(2,1)S(1)}, u32[]{:S(2)}, u32[]{:S(2)}) collective-permute-start(bf16[6,272,128]{2,1,0:T(8,128)(2,1)} %get-tuple-element.26), channel_id=1, source_target_pairs={{0,1},{1,0},{2,3},{3,2},{4,5},{5,4},{6,7},{7,6},{8,9},{9,8},{10,11... | collective-permute-start | bytes 1253384 | tf_op jit(solution)/shard_map/ppermute | solution.py:128
  168.9 31.7 %collective-permute-start.16 = (bf16[6,272,128]{2,1,0:T(8,128)(2,1)}, bf16[6,272,128]{2,1,0:T(8,128)(2,1)S(1)}, u32[]{:S(2)}, u32[]{:S(2)}) collective-permute-start(bf16[6,272,128]{2,1,0:T(8,128)(2,1)} %get-tuple-element.27), channel_id=1, source_target_pairs={{0,2},{1,3},{2,0},{3,1},{4,6},{5,7},{6,4},{7,5},{8,10},{9,11},{10,... | collective-permute-start | bytes 1253384 | tf_op jit(solution)/shard_map/ppermute | solution.py:128
  171.8 28.8 %collective-permute-start.17 = (bf16[6,272,128]{2,1,0:T(8,128)(2,1)}, bf16[6,272,128]{2,1,0:T(8,128)(2,1)S(1)}, u32[]{:S(2)}, u32[]{:S(2)}) collective-permute-start(bf16[6,272,128]{2,1,0:T(8,128)(2,1)} %get-tuple-element.28), channel_id=1, source_target_pairs={{0,3},{1,2},{2,1},{3,0},{4,7},{5,6},{6,5},{7,4},{8,11},{9,10},{10,... | collective-permute-start | bytes 1253384 | tf_op jit(solution)/shard_map/ppermute | solution.py:128
  236.7 17.7 %collective-permute-start.55 = (bf16[262,256]{1,0:T(8,128)(2,1)}, bf16[262,256]{1,0:T(8,128)(2,1)}, u32[]{:S(2)}, u32[]{:S(2)}) collective-permute-start(bf16[262,256]{1,0:T(8,128)(2,1)} %select_convert_fusion.8), channel_id=1, source_target_pairs={{0,8},{4,12},{8,0},{12,4},{16,24},{20,28},{24,16},{28,20},{1,9},{5... | collective-permute-start | bytes 402440 | tf_op jit(solution)/shard_map/ppermute | solution.py:44
  242.6 49.5 %collective-permute-start.41 = (bf16[6,272,128]{2,1,0:T(8,128)(2,1)}, bf16[6,272,128]{2,1,0:T(8,128)(2,1)}, u32[]{:S(2)}, u32[]{:S(2)}) collective-permute-start(bf16[6,272,128]{2,1,0:T(8,128)(2,1)} %concatenate.104.refs_8_), channel_id=1, source_target_pairs={{0,3},{1,2},{2,1},{3,0},{4,7},{5,6},{6,5},{7,4},{8,11},{9,10},{10,... | collective-permute-start | bytes 1253384 | tf_op jit(solution)/shard_map/ppermute | solution.py:62
  244.9 47.3 %collective-permute-start.40 = (bf16[6,272,128]{2,1,0:T(8,128)(2,1)}, bf16[6,272,128]{2,1,0:T(8,128)(2,1)}, u32[]{:S(2)}, u32[]{:S(2)}) collective-permute-start(bf16[6,272,128]{2,1,0:T(8,128)(2,1)} %concatenate.104.refs_8_), channel_id=1, source_target_pairs={{0,2},{1,3},{2,0},{3,1},{4,6},{5,7},{6,4},{7,5},{8,10},{9,11},{10,... | collective-permute-start | bytes 1253384 | tf_op jit(solution)/shard_map/ppermute | solution.py:62
  251.7 40.4 %collective-permute-start.39 = (bf16[6,272,128]{2,1,0:T(8,128)(2,1)}, bf16[6,272,128]{2,1,0:T(8,128)(2,1)}, u32[]{:S(2)}, u32[]{:S(2)}) collective-permute-start(bf16[6,272,128]{2,1,0:T(8,128)(2,1)} %concatenate.104.refs_8_), channel_id=1, source_target_pairs={{0,1},{1,0},{2,3},{3,2},{4,5},{5,4},{6,7},{7,6},{8,9},{9,8},{10,11... | collective-permute-start | bytes 1253384 | tf_op jit(solution)/shard_map/ppermute | solution.py:62
  256.8 9.1 %collective-permute-start.56 = (bf16[262,128]{1,0:T(8,128)(2,1)}, bf16[262,128]{1,0:T(8,128)(2,1)S(1)}, u32[]{:S(2)}, u32[]{:S(2)}) collective-permute-start(bf16[262,128]{1,0:T(8,128)(2,1)} %select_convert_fusion.11), channel_id=1, source_target_pairs={{0,16},{4,20},{8,24},{12,28},{16,0},{20,4},{24,8},{28,12},{1,17},{... | collective-permute-start | bytes 201224 | tf_op jit(solution)/shard_map/ppermute | solution.py:44
  267.0 8.8 %collective-permute-start.59 = (bf16[262,128]{1,0:T(8,128)(2,1)S(1)}, bf16[262,128]{1,0:T(8,128)(2,1)S(1)}, u32[]{:S(2)}, u32[]{:S(2)}) collective-permute-start(bf16[262,128]{1,0:T(8,128)(2,1)S(1)} %add_convert_fusion.3), channel_id=1, source_target_pairs={{0,3},{1,2},{2,1},{3,0},{4,7},{5,6},{6,5},{7,4},{8,11},{9,10},{10,... | collective-permute-start | bytes 201224 | tf_op jit(solution)/shard_map/ppermute | solution.py:62
  272.8 16.1 %collective-permute-start.58 = (bf16[262,128]{1,0:T(8,128)(2,1)S(1)}, bf16[262,128]{1,0:T(8,128)(2,1)S(1)}, u32[]{:S(2)}, u32[]{:S(2)}) collective-permute-start(bf16[262,128]{1,0:T(8,128)(2,1)S(1)} %add_convert_fusion.3), channel_id=1, source_target_pairs={{0,2},{1,3},{2,0},{3,1},{4,6},{5,7},{6,4},{7,5},{8,10},{9,11},{10,... | collective-permute-start | bytes 201224 | tf_op jit(solution)/shard_map/ppermute | solution.py:62
  275.8 14.6 %collective-permute-start.57 = (bf16[262,128]{1,0:T(8,128)(2,1)S(1)}, bf16[262,128]{1,0:T(8,128)(2,1)S(1)}, u32[]{:S(2)}, u32[]{:S(2)}) collective-permute-start(bf16[262,128]{1,0:T(8,128)(2,1)S(1)} %add_convert_fusion.3), channel_id=1, source_target_pairs={{0,1},{1,0},{2,3},{3,2},{4,5},{5,4},{6,7},{7,6},{8,9},{9,8},{10,11... | collective-permute-start | bytes 201224 | tf_op jit(solution)/shard_map/ppermute | solution.py:62
  288.9 68.7 %collective-permute-start.63 = (bf16[4,128,1024]{2,1,0:T(8,128)(2,1)S(1)}, bf16[4,128,1024]{2,1,0:T(8,128)(2,1)}, u32[]{:S(2)}, u32[]{:S(2)}) collective-permute-start(bf16[4,128,1024]{2,1,0:T(8,128)(2,1)S(1)} %fusion.56), channel_id=1, source_target_pairs={{0,4},{4,0},{8,12},{12,8},{16,20},{20,16},{24,28},{28,24},{1,5},{5... | collective-permute-start | bytes 3145736 | tf_op jit(solution)/shard_map/ppermute | solution.py:44
  290.4 26.2 %collective-permute-start.60 = (bf16[262,128]{1,0:T(8,128)(2,1)S(1)}, bf16[262,128]{1,0:T(8,128)(2,1)S(1)}, u32[]{:S(2)}, u32[]{:S(2)}) collective-permute-start(bf16[262,128]{1,0:T(8,128)(2,1)S(1)} %add_convert_fusion.2), channel_id=1, source_target_pairs={{0,16},{4,20},{8,24},{12,28},{16,0},{20,4},{24,8},{28,12},{1,17},{... | collective-permute-start | bytes 201224 | tf_op jit(solution)/shard_map/ppermute | solution.py:44
  312.1 17.9 %collective-permute-start.42 = (bf16[6,272,128]{2,1,0:T(8,128)(2,1)}, bf16[6,272,128]{2,1,0:T(8,128)(2,1)S(1)}, u32[]{:S(2)}, u32[]{:S(2)}) collective-permute-start(bf16[6,272,128]{2,1,0:T(8,128)(2,1)} %get-tuple-element.30), channel_id=1, source_target_pairs={{0,1},{1,0},{2,3},{3,2},{4,5},{5,4},{6,7},{7,6},{8,9},{9,8},{10,11... | collective-permute-start | bytes 1253384 | tf_op jit(solution)/shard_map/ppermute | solution.py:128
  314.1 31.6 %collective-permute-start.43 = (bf16[6,272,128]{2,1,0:T(8,128)(2,1)}, bf16[6,272,128]{2,1,0:T(8,128)(2,1)S(1)}, u32[]{:S(2)}, u32[]{:S(2)}) collective-permute-start(bf16[6,272,128]{2,1,0:T(8,128)(2,1)} %get-tuple-element.31), channel_id=1, source_target_pairs={{0,2},{1,3},{2,0},{3,1},{4,6},{5,7},{6,4},{7,5},{8,10},{9,11},{10,... | collective-permute-start | bytes 1253384 | tf_op jit(solution)/shard_map/ppermute | solution.py:128
  314.7 31.1 %collective-permute-start.44 = (bf16[6,272,128]{2,1,0:T(8,128)(2,1)}, bf16[6,272,128]{2,1,0:T(8,128)(2,1)S(1)}, u32[]{:S(2)}, u32[]{:S(2)}) collective-permute-start(bf16[6,272,128]{2,1,0:T(8,128)(2,1)} %get-tuple-element.32), channel_id=1, source_target_pairs={{0,3},{1,2},{2,1},{3,0},{4,7},{5,6},{6,5},{7,4},{8,11},{9,10},{10,... | collective-permute-start | bytes 1253384 | tf_op jit(solution)/shard_map/ppermute | solution.py:128
  321.8 52.9 %collective-permute-start.69 = (bf16[4,128,1024]{2,1,0:T(8,128)(2,1)S(1)}, bf16[4,128,1024]{2,1,0:T(8,128)(2,1)S(1)}, u32[]{:S(2)}, u32[]{:S(2)}) collective-permute-start(bf16[4,128,1024]{2,1,0:T(8,128)(2,1)S(1)} %fusion.57), channel_id=1, source_target_pairs={{0,4},{4,0},{8,12},{12,8},{16,20},{20,16},{24,28},{28,24},{1,5},{5... | collective-permute-start | bytes 3145736 | tf_op jit(solution)/shard_map/ppermute | solution.py:44
  329.9 22.4 %collective-permute-start.62 = (bf16[262,512]{1,0:T(8,128)(2,1)S(1)}, bf16[262,512]{1,0:T(8,128)(2,1)S(1)}, u32[]{:S(2)}, u32[]{:S(2)}) collective-permute-start(bf16[262,512]{1,0:T(8,128)(2,1)S(1)} %pad_maximum_fusion.16), channel_id=1, source_target_pairs={{0,4},{4,0},{8,12},{12,8},{16,20},{20,16},{24,28},{28,24},{1,5},{5... | collective-permute-start | bytes 804872 | tf_op jit(solution)/shard_map/ppermute | solution.py:44
  351.2 5.9 %collective-permute-start.46 = (bf16[261,256]{1,0:T(8,128)(2,1)S(1)}, bf16[261,256]{1,0:T(8,128)(2,1)S(1)}, u32[]{:S(2)}, u32[]{:S(2)}) collective-permute-start(bf16[261,256]{1,0:T(8,128)(2,1)S(1)} %select_convert_fusion.9), channel_id=1, source_target_pairs={{0,8},{4,12},{8,0},{12,4},{16,24},{20,28},{24,16},{28,20},{1,9},{5... | collective-permute-start | bytes 400904 | tf_op jit(solution)/shard_map/ppermute | solution.py:44
  361.6 9.5 %collective-permute-start.50 = (bf16[261,128]{1,0:T(8,128)(2,1)S(1)}, bf16[261,128]{1,0:T(8,128)(2,1)S(1)}, u32[]{:S(2)}, u32[]{:S(2)}) collective-permute-start(bf16[261,128]{1,0:T(8,128)(2,1)S(1)} %add_convert_fusion.5), channel_id=1, source_target_pairs={{0,3},{1,2},{2,1},{3,0},{4,7},{5,6},{6,5},{7,4},{8,11},{9,10},{10,... | collective-permute-start | bytes 200456 | tf_op jit(solution)/shard_map/ppermute | solution.py:62
  363.6 9.3 %collective-permute-start.49 = (bf16[261,128]{1,0:T(8,128)(2,1)S(1)}, bf16[261,128]{1,0:T(8,128)(2,1)S(1)}, u32[]{:S(2)}, u32[]{:S(2)}) collective-permute-start(bf16[261,128]{1,0:T(8,128)(2,1)S(1)} %add_convert_fusion.5), channel_id=1, source_target_pairs={{0,2},{1,3},{2,0},{3,1},{4,6},{5,7},{6,4},{7,5},{8,10},{9,11},{10,... | collective-permute-start | bytes 200456 | tf_op jit(solution)/shard_map/ppermute | solution.py:62
  370.0 18.0 %collective-permute-start.64 = (bf16[2,128,1024]{2,1,0:T(8,128)(2,1)S(1)}, bf16[2,128,1024]{2,1,0:T(8,128)(2,1)S(1)}, u32[]{:S(2)}, u32[]{:S(2)}) collective-permute-start(bf16[2,128,1024]{2,1,0:T(8,128)(2,1)S(1)} %fusion.79), channel_id=1, source_target_pairs={{0,8},{4,12},{8,0},{12,4},{16,24},{20,28},{24,16},{28,20},{1,9},{5... | collective-permute-start | bytes 1572872 | tf_op jit(solution)/shard_map/ppermute | solution.py:44
  378.6 9.2 %collective-permute-start.52 = (bf16[261,256]{1,0:T(8,128)(2,1)S(1)}, bf16[261,256]{1,0:T(8,128)(2,1)S(1)}, u32[]{:S(2)}, u32[]{:S(2)}) collective-permute-start(bf16[261,256]{1,0:T(8,128)(2,1)S(1)} %pad_maximum_fusion.28), channel_id=1, source_target_pairs={{0,8},{4,12},{8,0},{12,4},{16,24},{20,28},{24,16},{28,20},{1,9},{5... | collective-permute-start | bytes 400904 | tf_op jit(solution)/shard_map/ppermute | solution.py:44
  379.8 16.0 %collective-permute-start.70 = (bf16[2,128,1024]{2,1,0:T(8,128)(2,1)S(1)}, bf16[2,128,1024]{2,1,0:T(8,128)(2,1)S(1)}, u32[]{:S(2)}, u32[]{:S(2)}) collective-permute-start(bf16[2,128,1024]{2,1,0:T(8,128)(2,1)S(1)} %fusion.78), channel_id=1, source_target_pairs={{0,8},{4,12},{8,0},{12,4},{16,24},{20,28},{24,16},{28,20},{1,9},{5... | collective-permute-start | bytes 1572872 | tf_op jit(solution)/shard_map/ppermute | solution.py:44
  387.9 17.0 %collective-permute-start.53 = (bf16[261,512]{1,0:T(8,128)(2,1)S(1)}, bf16[261,512]{1,0:T(8,128)(2,1)S(1)}, u32[]{:S(2)}, u32[]{:S(2)}) collective-permute-start(bf16[261,512]{1,0:T(8,128)(2,1)S(1)} %pad_maximum_fusion.15), channel_id=1, source_target_pairs={{0,4},{4,0},{8,12},{12,8},{16,20},{20,16},{24,28},{28,24},{1,5},{5... | collective-permute-start | bytes 801800 | tf_op jit(solution)/shard_map/ppermute | solution.py:44
  388.3 9.2 %collective-permute-start.65 = (bf16[1,128,1024]{2,1,0:T(8,128)(2,1)S(1)}, bf16[1,128,1024]{2,1,0:T(8,128)(2,1)S(1)}, u32[]{:S(2)}, u32[]{:S(2)}) collective-permute-start(bf16[1,128,1024]{2,1,0:T(8,128)(2,1)S(1)} %fusion.80), channel_id=1, source_target_pairs={{0,16},{4,20},{8,24},{12,28},{16,0},{20,4},{24,8},{28,12},{1,17},{... | collective-permute-start | bytes 786440 | tf_op jit(solution)/shard_map/ppermute | solution.py:44
  396.2 6.5 %collective-permute-start.71 = (bf16[1,128,1024]{2,1,0:T(8,128)(2,1)S(1)}, bf16[1,128,1024]{2,1,0:T(8,128)(2,1)S(1)}, u32[]{:S(2)}, u32[]{:S(2)}) collective-permute-start(bf16[1,128,1024]{2,1,0:T(8,128)(2,1)S(1)} %fusion.81), channel_id=1, source_target_pairs={{0,16},{4,20},{8,24},{12,28},{16,0},{20,4},{24,8},{28,12},{1,17},{... | collective-permute-start | bytes 786440 | tf_op jit(solution)/shard_map/ppermute | solution.py:44
  397.6 14.7 %collective-permute-start.66 = (bf16[32,1024]{1,0:T(8,128)(2,1)S(1)}, bf16[32,1024]{1,0:T(8,128)(2,1)S(1)}, u32[]{:S(2)}, u32[]{:S(2)}) collective-permute-start(bf16[32,1024]{1,0:T(8,128)(2,1)S(1)} %get-tuple-element.76), channel_id=1, source_target_pairs={{0,1},{1,0},{2,3},{3,2},{4,5},{5,4},{6,7},{7,6},{8,9},{9,8},{10,11... | collective-permute-start | bytes 196616 | tf_op jit(solution)/shard_map/ppermute | solution.py:100
  399.7 12.6 %collective-permute-start.68 = (bf16[32,1024]{1,0:T(8,128)(2,1)S(1)}, bf16[32,1024]{1,0:T(8,128)(2,1)S(1)}, u32[]{:S(2)}, u32[]{:S(2)}) collective-permute-start(bf16[32,1024]{1,0:T(8,128)(2,1)S(1)} %get-tuple-element.77), channel_id=1, source_target_pairs={{0,3},{1,2},{2,1},{3,0},{4,7},{5,6},{6,5},{7,4},{8,11},{9,10},{10,... | collective-permute-start | bytes 196616 | tf_op jit(solution)/shard_map/ppermute | solution.py:100
  401.6 10.7 %collective-permute-start.67 = (bf16[32,1024]{1,0:T(8,128)(2,1)S(1)}, bf16[32,1024]{1,0:T(8,128)(2,1)S(1)}, u32[]{:S(2)}, u32[]{:S(2)}) collective-permute-start(bf16[32,1024]{1,0:T(8,128)(2,1)S(1)} %get-tuple-element.78), channel_id=1, source_target_pairs={{0,2},{1,3},{2,0},{3,1},{4,6},{5,7},{6,4},{7,5},{8,10},{9,11},{10,... | collective-permute-start | bytes 196616 | tf_op jit(solution)/shard_map/ppermute | solution.py:100
  402.9 10.2 %collective-permute-start.72 = (bf16[32,1024]{1,0:T(8,128)(2,1)S(1)}, bf16[32,1024]{1,0:T(8,128)(2,1)S(1)}, u32[]{:S(2)}, u32[]{:S(2)}) collective-permute-start(bf16[32,1024]{1,0:T(8,128)(2,1)S(1)} %get-tuple-element.73), channel_id=1, source_target_pairs={{0,1},{1,0},{2,3},{3,2},{4,5},{5,4},{6,7},{7,6},{8,9},{9,8},{10,11... | collective-permute-start | bytes 196616 | tf_op jit(solution)/shard_map/ppermute | solution.py:100
  404.9 8.1 %collective-permute-start.74 = (bf16[32,1024]{1,0:T(8,128)(2,1)S(1)}, bf16[32,1024]{1,0:T(8,128)(2,1)S(1)}, u32[]{:S(2)}, u32[]{:S(2)}) collective-permute-start(bf16[32,1024]{1,0:T(8,128)(2,1)S(1)} %get-tuple-element.74), channel_id=1, source_target_pairs={{0,3},{1,2},{2,1},{3,0},{4,7},{5,6},{6,5},{7,4},{8,11},{9,10},{10,... | collective-permute-start | bytes 196616 | tf_op jit(solution)/shard_map/ppermute | solution.py:100
  (78 other events, 703.1 us)
